TPU v7x, 256 devices: a whole 4x4x8 slice. The times are simulated.
256 devices in a mesh: slab: 32 (over z, x), pencil: 8 (over y, core).
Axes of the slice: x: 4, y: 4, z: 8, core: 2. Of those that a mesh axis runs over, the one named last changes fastest.
Arguments:
- vorticity: float32 [3, 256, 256, 256], P(None, 'slab', 'pencil')
- velocity: float32 [3, 256, 256, 256], P(None, 'slab', 'pencil'), may hold values from -6 to 6
- viscosity: float32 [256, 256, 256], P('slab', 'pencil'), may hold values from 0.02 to 0.4
- tile_weights: float32 [8192, 3, 128], P(('slab', 'pencil')), may hold values from -6 to 6
- tile_cells: int32 [8192, 128], P(('slab', 'pencil')), may hold values from 0 to 65535
- tile_dest: int32 [8192, 1], P(('slab', 'pencil')), may hold values from 0 to 31; in each aligned block of 32 rows (0 to 31, 32 to 63, ...) at most 2 rows name the same one
- tile_count: int32 [256], P(('slab', 'pencil')), may hold values from 8 to 32, as said below
Outputs:
- vorticity_out: float32 [3, 256, 256, 256], P(None, 'slab', 'pencil')
- far_velocity: float32 [3, 32, 8, 16], P(None, 'slab', 'pencil')
Inputs may be any that keep to these rules, and one draw needn't show every extreme that they name: Tiles of device (s, p) go to device (tile_dest, p). Among the 32 tiles of one device, at most 2 name one slab, a bound that some block reaches. The live tiles of a device are its first tile_count ones; some device has all 32 live.
All inputs are finite; a program needn't handle non-finite values.
Results may differ from a plain program's by a relative error of at most 0.0003.
Values sent between devices are 32-bit elements; how exact they have to be, the bound alone decides.
A program may use at most 128 MiB of HBM per device.

v0:
```python
import jax
import jax.numpy as jnp
from jax import lax
from jax.sharding import PartitionSpec as P

CB = 16
NCL = 16


time_step = 0.1


def with_halo(array, sides, width):
    for axis, dim in sides:
        devices, length = (lax.axis_size(axis), array.shape[dim])
        up = [(i, (i + 1) % devices) for i in range(devices - 1)]
        down = [(j, i) for i, j in up]
        last = lax.slice_in_dim(array, length - width, length, axis=dim)
        leading = lax.slice_in_dim(array, 0, width, axis=dim)
        before = lax.ppermute(last, axis, up)
        after = lax.ppermute(leading, axis, down)
        array = jnp.concatenate([before, array, after], axis=dim)
    return array


def interior(a):
    return a[..., 1:-1, 1:-1, :]


def ahead_x(a):
    return a[..., 2:, 1:-1, :]


def behind_x(a):
    return a[..., :-2, 1:-1, :]


def ahead_y(a):
    return a[..., 1:-1, 2:, :]


def behind_y(a):
    return a[..., 1:-1, :-2, :]


def ahead_z(a):
    return jnp.roll(interior(a), -1, axis=-1)


def behind_z(a):
    return jnp.roll(interior(a), 1, axis=-1)


def advance(padded):
    vort_all = padded[0:3]
    velo_all = padded[3:6]
    visc_all = padded[6]
    stencil_pairs = ((ahead_x, behind_x), (ahead_y, behind_y), (ahead_z, behind_z))
    own_vort = interior(vort_all)
    own_visc = interior(visc_all)
    stretch = jnp.zeros_like(own_vort)
    diffuse = jnp.zeros_like(own_vort)
    for axis_num in range(3):
        forward, backward = stencil_pairs[axis_num]
        stretch = stretch + own_vort[axis_num] * (0.5 * (forward(velo_all) - backward(velo_all)))
        for neighbour in stencil_pairs[axis_num]:
            diffuse = diffuse + 0.5 * (own_visc + neighbour(visc_all)) * (
                neighbour(vort_all) - own_vort
            )
    return own_vort + time_step * (stretch + diffuse)


def centres(cols, cx, cy, cb, npencil, ncl):
    slab_idx = cols // (npencil * ncl)
    pencil_idx = cols // ncl % npencil
    level = cols % ncl
    xpos = (slab_idx * cx).astype(jnp.float32) + (cx - 1) * 0.5
    ypos = (pencil_idx * cy).astype(jnp.float32) + (cy - 1) * 0.5
    zpos = (level * cb).astype(jnp.float32) + (cb - 1) * 0.5
    return (xpos, ypos, zpos)


def far_terms(targets, sources, moments, sigma):
    high = lax.Precision.HIGHEST
    rel_x = targets[0][:, None] - sources[0][None, :]
    rel_y = targets[1][:, None] - sources[1][None, :]
    rel_z = targets[2][:, None] - sources[2][None, :]
    dist_sq = rel_x * rel_x + rel_y * rel_y + rel_z * rel_z + sigma * sigma
    inverse = lax.rsqrt(dist_sq)
    weight = inverse * inverse * inverse
    trans = moments.T
    along_x = jnp.dot(weight * rel_x, trans, precision=high)
    along_y = jnp.dot(weight * rel_y, trans, precision=high)
    along_z = jnp.dot(weight * rel_z, trans, precision=high)
    first = along_z[:, 1] - along_y[:, 2]
    second = along_x[:, 2] - along_z[:, 0]
    third = along_y[:, 0] - along_x[:, 1]
    return jnp.stack([first, second, third], 0)


def deposit(field_flat, weights, local_cells):
    values = jnp.transpose(weights, (1, 0, 2)).reshape(3, -1)
    return field_flat.at[:, local_cells.reshape(-1)].add(values)


def per_device(vorticity, velocity, viscosity, tile_weights, tile_cells, tile_dest, tile_count):
    cx_dev = vorticity.shape[1]
    cy_dev = vorticity.shape[2]
    nz_all = vorticity.shape[3]
    cells_dev = cx_dev * cy_dev * nz_all
    tiles_dev = tile_weights.shape[0]
    tile_len = tile_weights.shape[2]
    n_slab = lax.axis_size("slab")
    n_pencil = lax.axis_size("pencil")
    stacked = jnp.concatenate([vorticity, velocity, viscosity[None]], 0)
    padded = with_halo(stacked, (("slab", 1), ("pencil", 2)), 1)
    advanced = advance(padded)
    field = advanced.reshape(3, cells_dev)
    live = (jnp.arange(tiles_dev, dtype=jnp.int32) < tile_count[0]).astype(jnp.float32)
    live_weights = tile_weights * live[:, None, None]
    dest = tile_dest[:, 0]
    coded = (tile_cells + dest[:, None] * cells_dev).astype(jnp.float32)
    payload = jnp.concatenate([live_weights, coded[:, None, :]], 1)
    arrived = lax.all_gather(payload, "slab", axis=0, tiled=True)
    code_int = arrived[:, 3, :].astype(jnp.int32)
    row_target = code_int[:, 0] // cells_dev
    local_cells = code_int - row_target[:, None] * cells_dev
    keep_row = row_target == lax.axis_index("slab")
    rows_kept = 2 * tiles_dev
    position = jnp.cumsum(keep_row.astype(jnp.int32)) - 1
    position = jnp.where(keep_row, position, rows_kept)
    compact_weights = (
        jnp.zeros((rows_kept, 3, tile_len), jnp.float32)
        .at[position]
        .set(arrived[:, 0:3, :], mode="drop")
    )
    compact_cells = (
        jnp.zeros((rows_kept, tile_len), jnp.int32).at[position].set(local_cells, mode="drop")
    )
    field = deposit(field, compact_weights, compact_cells)
    vorticity_out = field.reshape(3, cx_dev, cy_dev, nz_all)
    moment = vorticity_out.reshape(3, cx_dev, cy_dev, NCL, CB).sum(axis=(1, 2, 4))
    sigma = jnp.float32(cx_dev * n_slab // 4)
    own_cols = (lax.axis_index("slab") * n_pencil + lax.axis_index("pencil")) * NCL + jnp.arange(
        NCL, dtype=jnp.int32
    )
    targets = centres(own_cols, cx_dev, cy_dev, CB, n_pencil, NCL)
    piece = lax.all_gather(moment, ("slab", "pencil"), axis=1, tiled=True)
    cols = jnp.arange(piece.shape[1], dtype=jnp.int32)
    sources = centres(cols, cx_dev, cy_dev, CB, n_pencil, NCL)
    far_local = far_terms(targets, sources, piece, sigma)
    far_velocity = far_local.reshape(3, 1, 1, NCL)
    return (vorticity_out, far_velocity)


def solution(mesh):
    in_specs = (
        P(None, "slab", "pencil", None),
        P(None, "slab", "pencil", None),
        P("slab", "pencil", None),
        P(("slab", "pencil"), None, None),
        P(("slab", "pencil"), None),
        P(("slab", "pencil"), None),
        P(("slab", "pencil")),
    )
    out_specs = (P(None, "slab", "pencil", None), P(None, "slab", "pencil", None))
    return jax.shard_map(
        per_device, mesh=mesh, in_specs=in_specs, out_specs=out_specs, check_vma=False
    )
```

profile of v0, /device:TPU:1, one launch (start us, length us, event | category | flops | bytes accessed | tf_op | source)
XLA Modules:
  0.0 315.0 jit_solution(2625327712452044664)
XLA Ops:
  7.2 0.0 copy-start
  7.2 0.0 copy-start.1
  7.2 0.0 all-gather.3.cloned.1.call-start
  8.0 0.7 multiply_bitcast_fusion.3
  8.7 0.9 broadcast_multiply_fusion
  9.5 0.8 convert_bitcast_fusion
  10.3 0.6 pad_maximum_fusion.30
  11.0 0.0 all-gather.3.cloned.1.call-update
  11.0 1.1 pad_maximum_fusion.22
  12.1 1.3 collective-permute-start
  13.4 4.6 %collective-permute-start.1 = (f32[7,1,32,256]{3,2,1,0:T(8,128)S(1)}, f32[7,1,32,256]{3,2,1,0:T(8,128)S(1)}, u32[]{:S(2)}, u32[]{:S(2)}) collective-permute-start(f32[7,1,32,256]{3,2,1,0:T(8,128)S(1)} %get-tuple-element.16), channel_id=1, source_target_pairs={{0,8},{8,16},{16,24},{24,32},{32,40},{40,48},{48,56},{56,64},{64,7... | collective-permute-start | bytes 688136 | tf_op jit(solution)/shard_map/ppermute | solution.py:20
  18.1 0.0 copy-done
  18.1 0.0 copy-done.1
  18.1 0.3 fusion.101
  18.4 0.0 copy-start.3
  18.4 0.5 fusion.102
  18.9 0.1 multiply_bitcast_fusion.2
  19.0 0.4 collective-permute-done
  19.5 1.5 collective-permute-done.1
  20.9 0.0 copy-done.3
  20.9 0.1 pad_maximum_fusion.29
  21.1 5.7 %collective-permute-start.2 = (f32[7,10,1,256]{3,0,2,1:T(8,128)S(1)}, f32[7,10,1,256]{3,0,2,1:T(8,128)S(1)}, u32[]{:S(2)}, u32[]{:S(2)}) collective-permute-start(f32[7,10,1,256]{3,0,2,1:T(8,128)S(1)} %copy.51), channel_id=1, source_target_pairs={{1,0},{2,1},{3,2},{4,3},{5,4},{6,5},{7,6},{9,8},{10,9},{11,10},{12... | collective-permute-start | bytes 215048 | tf_op jit(solution)/shard_map/ppermute | solution.py:21
  26.8 2.4 collective-permute-start.3
  29.2 0.1 collective-permute-done.2
  29.4 0.1 copy.52
  29.4 1.2 collective-permute-done.3
  30.7 0.1 copy.54
  30.7 0.1 fusion.29
  30.8 0.1 fusion.106
  30.9 0.1 fusion.105
  31.0 0.2 fusion.40
  31.3 3.7 %fusion.7 = f32[3,8,32,256]{3,2,1,0:T(8,128)S(1)} fusion(f32[3,8,32,256]{3,2,1,0:T(8,128)S(1)} %copy-done, f32[7,10,1,256]{3,2,1,0:T(1,128)S(1)} %copy.54, f32[7,1,32,256]{3,2,1,0:T(8,128)S(1)} %collective-permute-done, f32[7,1,32,256]{3,2,1,0:T(8,128)S(1)} %collective-permute-done.1, f32[1,8,32,256]{3,2,1,0:T(8,128)S(1)} %bitcast.71, ...), kind=kLoop, calls=%fused_computation.12 | loop fusion | flops 12582912 | bytes 8728576 | tf_op jit(solution)/shard_map/add | solution.py:70
  35.0 16.6 %copy.57 = f32[3,8,32,256]{0,3,2,1:T(8,128)} copy(f32[3,8,32,256]{3,2,1,0:T(8,128)S(1)} %fusion.7) | data formatting | bytes 1572864 | tf_op jit(solution)/shard_map/add | solution.py:70
  51.6 37.4 %all-gather.3.cloned.1.call-done = f32[1024,4,128]{2,0,1:T(8,128)} async-done(((f32[32,4,128]{2,0,1:T(8,128)}), f32[1024,4,128]{2,0,1:T(8,128)}) %all-gather.3.cloned.1.call-update) | async-done | bytes 2097168 | tf_op jit(solution)/shard_map/all_gather | solution.py:124
  89.0 0.0 copy-start.2
  89.0 1.2 fusion.25
  90.2 0.5 multiply_reduce_fusion
  90.8 0.3 reduce-window.9
  91.1 0.1 slice.229
  91.2 0.1 slice_reduce_fusion.1
  91.3 0.1 add_add_fusion
  91.3 0.2 copy.58
  91.6 0.5 fusion.24
  92.1 0.0 copy-done.2
  92.1 3.6 %scatter_custom_fusion = s32[64,128]{1,0:T(8,128)S(1)} fusion(s32[1024]{0:T(1024)S(1)} %fusion.24, s32[1024]{0:T(1024)S(1)} %get-tuple-element.12, s32[]{:T(128)} %constant.124.clone.1, f32[1024,4,128]{2,0,1:T(8,128)S(1)} %copy-done.2), kind=kCustom, calls=%fused_computation.56 | custom fusion | flops 262144 | bytes 561156 | tf_op jit(solution)/shard_map/scatter | solution.py:138
  95.7 0.0 slice-start
  95.8 1.4 slice-done
  97.1 1.1 copy.59
  98.2 29.2 %scatter_fusion = f32[64,3,128]{2,1,0:T(4,128)S(1)} fusion(f32[64,3,128]{2,1,0:T(4,128)S(1)} %broadcast_in_dim.16, s32[1024]{0:T(1024)S(1)} %fusion.24, f32[1024,3,128]{2,1,0:T(4,128)S(1)} %copy.59), kind=kCustom, calls=%fused_computation.1 | custom fusion | bytes 4722688 | tf_op jit(solution)/shard_map/scatter | solution.py:135
  127.4 2.7 copy.60
  130.2 70.1 %scatter_fusion.1 = f32[3,65536]{0,1:T(8,128)} fusion(f32[3,65536]{0,1:T(8,128)} %bitcast.64, s32[8192]{0:T(1024)S(1)} %bitcast.72, f32[8192,3]{1,0:T(8,128)} %copy.60), kind=kCustom, calls=%fused_computation.2 | custom fusion | flops 24576 | bytes 327680 | tf_op jit(solution)/shard_map/scatter-add | solution.py:103
  200.3 13.2 %reduce_sum.9 = f32[3,16]{0,1:T(8,128)S(1)} reduce(f32[3,8,32,16,16]{0,4,3,2,1:T(8,128)} %bitcast.65, f32[]{:T(128)} %constant.133.clone.1), dimensions={1,2,4}, to_apply=%region_5.6 | reduce | flops 196560 | bytes 786628 | tf_op jit(solution)/shard_map/reduce_sum | solution.py:142
  213.5 0.1 copy.61
  213.5 71.8 %all-gather = f32[256,16,3]{1,2,0:T(4,128)S(1)} all-gather(f32[1,16,3]{1,2,0:T(4,128)S(1)} %bitcast.76), channel_id=1, replica_groups=mesh['slab'=32,'pencil'=8] {'slab','pencil'}, dimensions={0}, use_global_device_ids=true | all-gather | bytes 49344 | tf_op jit(solution)/shard_map/all_gather | solution.py:148
  285.4 0.2 reshape.311
  285.6 0.5 fusion.34
  286.2 0.6 fusion.35
  286.7 0.6 fusion.36
  287.4 0.6 copy.64
  287.9 20.2 %copy.63 = f32[3,8,32,256]{3,2,1,0:T(8,128)} copy(f32[3,8,32,256]{0,3,2,1:T(8,128)} %bitcast.66) | data formatting | bytes 1572864
  (14 shorter events, 0.2 us)
Async XLA Ops:
  7.2 10.9 %copy-start = (f32[3,8,32,256]{3,2,1,0:T(8,128)S(1)}, f32[3,8,32,256]{3,2,1,0:T(8,128)}, u32[]{:S(2)}) copy-start(f32[3,8,32,256]{3,2,1,0:T(8,128)} %param.7) | copy-start | bytes 2359300
  7.2 10.9 %copy-start.1 = (f32[3,8,32,256]{3,2,1,0:T(8,128)S(1)}, f32[3,8,32,256]{3,2,1,0:T(8,128)}, u32[]{:S(2)}) copy-start(f32[3,8,32,256]{3,2,1,0:T(8,128)} %param.8) | copy-start | bytes 2359300
  7.2 81.8 %all-gather.3.cloned.1.call-start = ((), (), s32[]{:S(2)}) async-start(), calls=%async_computation | async-start | bytes 2162688 | tf_op jit(solution)/shard_map/all_gather | solution.py:124
  12.1 7.4 %collective-permute-start = (f32[7,1,32,256]{3,2,1,0:T(8,128)S(1)}, f32[7,1,32,256]{3,2,1,0:T(8,128)S(1)}, u32[]{:S(2)}, u32[]{:S(2)}) collective-permute-start(f32[7,1,32,256]{3,2,1,0:T(8,128)S(1)} %get-tuple-element.17), channel_id=1, source_target_pairs={{8,0},{16,8},{24,16},{32,24},{40,32},{48,40},{56,48},{64,56},{72,6... | collective-permute-start | bytes 688136 | tf_op jit(solution)/shard_map/ppermute | solution.py:21
  13.4 7.5 %collective-permute-start.1 = (f32[7,1,32,256]{3,2,1,0:T(8,128)S(1)}, f32[7,1,32,256]{3,2,1,0:T(8,128)S(1)}, u32[]{:S(2)}, u32[]{:S(2)}) collective-permute-start(f32[7,1,32,256]{3,2,1,0:T(8,128)S(1)} %get-tuple-element.16), channel_id=1, source_target_pairs={{0,8},{8,16},{16,24},{24,32},{32,40},{40,48},{48,56},{56,64},{64,7... | collective-permute-start | bytes 688136 | tf_op jit(solution)/shard_map/ppermute | solution.py:20
  18.4 2.6 copy-start.3
  21.1 8.3 %collective-permute-start.2 = (f32[7,10,1,256]{3,0,2,1:T(8,128)S(1)}, f32[7,10,1,256]{3,0,2,1:T(8,128)S(1)}, u32[]{:S(2)}, u32[]{:S(2)}) collective-permute-start(f32[7,10,1,256]{3,0,2,1:T(8,128)S(1)} %copy.51), channel_id=1, source_target_pairs={{1,0},{2,1},{3,2},{4,3},{5,4},{6,5},{7,6},{9,8},{10,9},{11,10},{12... | collective-permute-start | bytes 215048 | tf_op jit(solution)/shard_map/ppermute | solution.py:21
  26.8 3.9 %collective-permute-start.3 = (f32[7,10,1,256]{3,0,2,1:T(8,128)S(1)}, f32[7,10,1,256]{3,0,2,1:T(8,128)S(1)}, u32[]{:S(2)}, u32[]{:S(2)}) collective-permute-start(f32[7,10,1,256]{3,0,2,1:T(8,128)S(1)} %copy.53), channel_id=1, source_target_pairs={{0,1},{1,2},{2,3},{3,4},{4,5},{5,6},{6,7},{8,9},{9,10},{10,11},{11... | collective-permute-start | bytes 215048 | tf_op jit(solution)/shard_map/ppermute | solution.py:20
  89.0 3.1 copy-start.2
  95.7 1.4 slice-start
Sparse Core Ops, SparseCore 0:
  11.2 77.7 all-gather.2
where the time goes:
time: 316 us; the launch traced here: 315 us
  other arithmetic  97.9 us (31%)
  local copies, waits for them, and re-layouts  73.8 us (23%)
  blocking collectives  71.8 us (23%)
  waiting for transfers between devices  40.6 us (13%)
  between operations  15.1 us (5%)
  starting transfers between devices  14 us (4%)
    all_gather x1, blocking collectives, per_device(): piece = lax.all_gather(moment, ('slab', 'pencil'), axis=1, tiled=True)  71.8 us
    scatter-add x1, other arithmetic, deposit(): return field_flat.at[:, local_cells.reshape(-1)].add(values)  70.1 us
    all_gather x1, waiting for transfers between devices, per_device(): arrived = lax.all_gather(payload, 'slab', axis=0, tiled=True)  37.4 us
    scatter x1, local copies, waits for them, and re-layouts, per_device(): compact_weights = jnp.zeros((rows_kept, 3, tile_len), jnp.float32).at[pos...  29.2 us
    unnamed x12, local copies, waits for them, and re-layouts  21.1 us
    add x1, local copies, waits for them, and re-layouts, advance(): return own_vort + time_step * (stretch + diffuse)  16.6 us
    reduce_sum x1, other arithmetic, per_device(): vorticity_out.reshape(3, cx_dev, cy_dev, NCL, CB).sum(axis=(1, 2, 4))  13.2 us
    ppermute x2, starting transfers between devices, with_halo(): before = lax.ppermute(last, axis, up)  7 us
  transfers between devices with their start and end apart: 5, of which 5 were waited for; matrix products, arithmetic and copies ran while one was open for 7% of the time, Pallas kernels for 0%

commit v1 on v0

v1 whole, which is shorter than its diff:
```python
import functools

import jax
import jax.numpy as jnp
from jax import lax
from jax.experimental import pallas as pl
from jax.experimental.pallas import tpu as pltpu
from jax.sharding import PartitionSpec as P

CB = 16
FIELDS = 7
time_step = 0.1
HIGH = lax.Precision.HIGHEST
F32 = jnp.float32
BF16 = jnp.bfloat16
MESH = pl.DeviceIdType.MESH


def iota(shape, dim):
    return lax.broadcasted_iota(jnp.int32, shape, dim)


def signal_peers(axis, me, count, offsets):
    barrier = pltpu.get_barrier_semaphore()

    def one(k, carry):
        peer = lax.rem(me + k, count)
        pl.semaphore_signal(barrier, inc=1, device_id={axis: peer}, device_id_type=MESH)
        return carry

    lax.fori_loop(offsets[0], offsets[1], one, 0)


def remote(src, dst, send_sem, recv_sem, device):
    return pltpu.make_async_remote_copy(
        src_ref=src, dst_ref=dst, send_sem=send_sem, recv_sem=recv_sem, device_id=device, device_id_type=MESH
    )


def pack_tiles(weights, cells, dest, live, send, n_slab):
    tiles = cells.shape[0]
    slab = iota((n_slab, tiles), 0)
    tile = iota((n_slab, tiles), 1)
    match = jnp.where((dest[...] == slab) & (tile < live), 1.0, 0.0)
    earlier = jnp.where(iota((tiles, tiles), 0) < iota((tiles, tiles), 1), 1.0, 0.0)
    before = jnp.dot(match, earlier, preferred_element_type=F32)
    for j in range(2):
        pick = jnp.where(before == j, match, 0.0)
        for c in range(4):
            rows = weights[c] if c < 3 else (cells[...] + 1).astype(F32)
            send[:, 4 * j + c, :] = jnp.dot(pick, rows, precision=HIGH, preferred_element_type=F32)


def exchange_kernel(
    n_slab, n_pencil, vort, velo, visc, weights, cells, dest, count,
    tiles, xhalo, yhalo, field, send, yface, load_sem, xsend, xrecv, ysend, yrecv, tsend, trecv,
):
    slab, pencil = lax.axis_index("slab"), lax.axis_index("pencil")
    cx, cy = field.shape[1], field.shape[2]
    barrier = pltpu.get_barrier_semaphore()
    signal_peers("slab", slab, n_slab, (1, n_slab))
    p_up, p_down = lax.rem(pencil + 1, n_pencil), lax.rem(pencil + n_pencil - 1, n_pencil)
    for peer in (p_up, p_down):
        pl.semaphore_signal(barrier, inc=1, device_id={"pencil": peer}, device_id_type=MESH)
    loads = [
        pltpu.make_async_copy(vort, field.at[0:3], load_sem.at[0]),
        pltpu.make_async_copy(velo, field.at[3:6], load_sem.at[1]),
        pltpu.make_async_copy(visc, field.at[6], load_sem.at[2]),
    ]
    for load in loads:
        load.start()
    pack_tiles(weights, cells, dest, count[0], send, n_slab)
    for load in loads:
        load.wait()
    for c in range(FIELDS):
        yface[0, c] = field[c, :, 0, :]
        yface[1, c] = field[c, :, cy - 1, :]
    pl.semaphore_wait(barrier, n_slab - 1 + 2)

    s_up, s_down = lax.rem(slab + 1, n_slab), lax.rem(slab + n_slab - 1, n_slab)
    halos = [
        remote(field.at[:, 0], xhalo.at[1], xsend.at[0], xrecv.at[1], {"slab": s_down}),
        remote(field.at[:, cx - 1], xhalo.at[0], xsend.at[1], xrecv.at[0], {"slab": s_up}),
        remote(yface.at[0], yhalo.at[1], ysend.at[0], yrecv.at[1], {"pencil": p_down}),
        remote(yface.at[1], yhalo.at[0], ysend.at[1], yrecv.at[0], {"pencil": p_up}),
    ]
    for halo in halos:
        halo.start()

    def deliver(k, carry):
        peer = lax.rem(slab + k, n_slab)
        remote(send.at[peer], tiles.at[k], tsend, trecv, {"slab": peer}).start()
        return carry

    lax.fori_loop(1, n_slab, deliver, 0)
    tiles[0] = send[slab]
    everything = remote(send.at[1:n_slab], tiles.at[1:n_slab], tsend, trecv, {"slab": s_up})
    everything.wait_send()
    everything.wait_recv()
    for halo in halos:
        halo.wait()


def deposit(tiles, lhs, rhs, total):
    rows, nz = total.shape[0] // 3, total.shape[1]
    width = 2 * tiles.shape[2]
    shift = nz.bit_length() - 1
    number = iota((rows, width), 0).astype(F32).astype(BF16)
    total[...] = jnp.zeros_like(total)

    def add(i, carry):
        tile = tiles[i]
        entry = [jnp.concatenate([tile[c : c + 1], tile[4 + c : 5 + c]], axis=1) for c in range(4)]
        cell = entry[3].astype(jnp.int32) - 1
        high = (cell >> shift).astype(F32).astype(BF16)
        low = (cell & (nz - 1)).astype(F32).astype(BF16)
        here = number == high
        for c in range(3):
            first = entry[c].astype(BF16)
            second = (entry[c] - first.astype(F32)).astype(BF16)
            lhs[c * rows : (c + 1) * rows, 0:width] = jnp.where(here, first, jnp.zeros_like(first))
            lhs[c * rows : (c + 1) * rows, width : 2 * width] = jnp.where(here, second, jnp.zeros_like(second))
        onehot = jnp.where(number == low, jnp.ones((), BF16), jnp.zeros((), BF16))
        rhs[:, 0:width] = onehot
        rhs[:, width : 2 * width] = onehot
        total[...] += lax.dot_general(
            lhs[...], rhs[...], (((1,), (1,)), ((), ())), preferred_element_type=F32
        )
        return carry

    lax.fori_loop(0, tiles.shape[0], add, 0)


def block_kernel(
    n_slab, n_pencil, vort, velo, visc, xhalo, yhalo, tiles, out, moment, field, lhs, rhs, total, load_sem
):
    slab, pencil = lax.axis_index("slab"), lax.axis_index("pencil")
    cx, cy, nz = out.shape[1], out.shape[2], out.shape[3]
    loads = [
        pltpu.make_async_copy(vort, field.at[0:3, 1 : cx + 1], load_sem.at[0]),
        pltpu.make_async_copy(velo, field.at[3:6, 1 : cx + 1], load_sem.at[1]),
        pltpu.make_async_copy(visc, field.at[6, 1 : cx + 1], load_sem.at[2]),
    ]
    for load in loads:
        load.start()
    field[:, 0] = jnp.where(slab > 0, xhalo[0], 0.0)
    field[:, cx + 1] = jnp.where(slab < n_slab - 1, xhalo[1], 0.0)
    deposit(tiles, lhs, rhs, total)
    for load in loads:
        load.wait()
    row = iota((cy, nz), 0)
    first_row, last_row = row == 0, row == cy - 1
    has_before, has_after = pencil > 0, pencil < n_pencil - 1

    def plane(x, sums):
        def ahead_y(c):
            edge = jnp.where(has_after, yhalo[1, c, pl.ds(x, 1), :], 0.0)
            return jnp.where(last_row, edge, pltpu.roll(field[c, x + 1], cy - 1, 0))

        def behind_y(c):
            edge = jnp.where(has_before, yhalo[0, c, pl.ds(x, 1), :], 0.0)
            return jnp.where(first_row, edge, pltpu.roll(field[c, x + 1], 1, 0))

        neighbours = [
            (lambda c: field[c, x + 2], lambda c: field[c, x]),
            (ahead_y, behind_y),
            (lambda c: pltpu.roll(field[c, x + 1], nz - 1, 1), lambda c: pltpu.roll(field[c, x + 1], 1, 1)),
        ]
        own = [field[c, x + 1] for c in range(3)]
        own_visc = field[6, x + 1]
        change = [jnp.zeros_like(own_visc) for c in range(3)]
        for d, (forward, backward) in enumerate(neighbours):
            factor = 0.5 * own[d]
            face_ahead = 0.5 * (own_visc + forward(6))
            face_behind = 0.5 * (own_visc + backward(6))
            for c in range(3):
                change[c] += factor * (forward(3 + c) - backward(3 + c))
                change[c] += face_ahead * (forward(c) - own[c])
                change[c] += face_behind * (backward(c) - own[c])
        result = []
        for c in range(3):
            start = pl.multiple_of(c * cx * cy + x * cy, cy)
            value = own[c] + time_step * change[c] + total[pl.ds(start, cy), :]
            out[c, x] = value
            result.append(sums[c] + jnp.sum(value, axis=0, keepdims=True))
        return tuple(result)

    sums = lax.fori_loop(0, cx, plane, tuple(jnp.zeros((1, nz), F32) for c in range(3)))
    lanes = moment.shape[1]
    levels = nz // CB
    group = jnp.where(iota((nz, lanes), 0) // CB + pencil * levels == iota((nz, lanes), 1), 1.0, 0.0)
    stacked = jnp.concatenate(list(sums) + [jnp.zeros((5, nz), F32)], axis=0)
    moment[...] = jnp.dot(stacked, group, precision=HIGH, preferred_element_type=F32)


def far_kernel(
    n_slab, n_pencil, cx, cy, sigma, moment, out, inbox, slab_moment, everywhere, asend, arecv, bsend, brecv
):
    slab, pencil = lax.axis_index("slab"), lax.axis_index("pencil")
    barrier = pltpu.get_barrier_semaphore()
    signal_peers("pencil", pencil, n_pencil, (1, n_pencil))
    signal_peers("slab", slab, n_slab, (1, n_slab))
    pl.semaphore_wait(barrier, n_slab - 1 + n_pencil - 1)

    def to_pencil(k, carry):
        remote(moment, inbox.at[k], asend, arecv, {"pencil": lax.rem(pencil + k, n_pencil)}).start()
        return carry

    lax.fori_loop(1, n_pencil, to_pencil, 0)
    inbox[0] = moment[...]
    arrived = remote(inbox.at[1:n_pencil], inbox.at[1:n_pencil], asend, arecv, {"pencil": lax.rem(pencil + 1, n_pencil)})
    arrived.wait_recv()
    slab_moment[...] = jnp.sum(inbox[...], axis=0)

    def to_slab(k, carry):
        peer = lax.rem(slab + k, n_slab)
        remote(slab_moment, everywhere.at[slab], bsend, brecv, {"slab": peer}).start()
        return carry

    lax.fori_loop(1, n_slab, to_slab, 0)
    everywhere[slab] = slab_moment[...]
    gathered = remote(
        everywhere.at[1:n_slab], everywhere.at[1:n_slab], bsend, brecv, {"slab": lax.rem(slab + 1, n_slab)}
    )
    gathered.wait_recv()
    arrived.wait_send()
    gathered.wait_send()

    lanes = moment.shape[1]
    levels = lanes // n_pencil
    shape = (n_slab, lanes)
    rel_x = ((slab - iota(shape, 0)) * cx).astype(F32)
    rel_y = ((pencil - iota(shape, 1) // levels) * cy).astype(F32)
    level = iota(shape, 1) % levels
    plane_sq = rel_x * rel_x + rel_y * rel_y + sigma * sigma
    m0, m1, m2 = (everywhere[:, c, :] for c in range(3))
    fixed = (-(rel_y * m2), rel_x * m2, rel_y * m0 - rel_x * m1)
    sums = ([], [], [])
    for target in range(levels):
        rel_z = ((target - level) * CB).astype(F32)
        inverse = lax.rsqrt(plane_sq + rel_z * rel_z)
        weight = inverse * inverse * inverse
        terms = (rel_z * m1 + fixed[0], fixed[1] - rel_z * m0, fixed[2])
        for c in range(3):
            sums[c].append(jnp.sum(weight * terms[c], axis=0, keepdims=True))
    ones = jnp.ones((8, lanes), F32)
    for c in range(3):
        rows = jnp.concatenate(sums[c], axis=0)
        out[c, 0] = lax.dot_general(
            ones, rows, (((1,), (1,)), ((), ())), precision=HIGH, preferred_element_type=F32
        )[0:1]


def per_device(n_slab, n_pencil, vorticity, velocity, viscosity, tile_weights, tile_cells, tile_dest, tile_count):
    _, cx, cy, nz = vorticity.shape
    tile_len = tile_weights.shape[2]
    levels = nz // CB
    lanes = n_pencil * levels
    hbm = pl.BlockSpec(memory_space=pl.ANY)
    vmem = pl.BlockSpec(memory_space=pltpu.VMEM)
    smem = pl.BlockSpec(memory_space=pltpu.SMEM)
    dma = pltpu.SemaphoreType.DMA
    tiles, xhalo, yhalo = pl.pallas_call(
        functools.partial(exchange_kernel, n_slab, n_pencil),
        out_shape=(
            jax.ShapeDtypeStruct((n_slab, 8, tile_len), F32),
            jax.ShapeDtypeStruct((2, FIELDS, cy, nz), F32),
            jax.ShapeDtypeStruct((2, FIELDS, cx, nz), F32),
        ),
        in_specs=[hbm, hbm, hbm, vmem, vmem, vmem, smem],
        out_specs=(vmem, vmem, vmem),
        scratch_shapes=[
            pltpu.VMEM((FIELDS, cx, cy, nz), F32),
            pltpu.VMEM((n_slab, 8, tile_len), F32),
            pltpu.VMEM((2, FIELDS, cx, nz), F32),
            dma((3,)), dma((2,)), dma((2,)), dma((2,)), dma((2,)), dma, dma,
        ],
        compiler_params=pltpu.CompilerParams(collective_id=0, has_side_effects=True, vmem_limit_bytes=24 << 20),
        name="exchange",
    )(vorticity, velocity, viscosity, jnp.transpose(tile_weights, (1, 0, 2)), tile_cells, tile_dest.reshape(1, -1), tile_count)
    vorticity_out, moment = pl.pallas_call(
        functools.partial(block_kernel, n_slab, n_pencil),
        out_shape=(
            jax.ShapeDtypeStruct(vorticity.shape, F32),
            jax.ShapeDtypeStruct((8, lanes), F32),
        ),
        in_specs=[hbm, hbm, hbm, vmem, vmem, vmem],
        out_specs=(vmem, vmem),
        scratch_shapes=[
            pltpu.VMEM((FIELDS, cx + 2, cy, nz), F32),
            pltpu.VMEM((3 * cx * cy, 4 * tile_len), BF16),
            pltpu.VMEM((nz, 4 * tile_len), BF16),
            pltpu.VMEM((3 * cx * cy, nz), F32),
            dma((3,)),
        ],
        compiler_params=pltpu.CompilerParams(vmem_limit_bytes=40 << 20),
        name="block",
    )(vorticity, velocity, viscosity, xhalo, yhalo, tiles)
    far_velocity = pl.pallas_call(
        functools.partial(far_kernel, n_slab, n_pencil, cx, cy, float(cx * n_slab // 4)),
        out_shape=jax.ShapeDtypeStruct((3, 1, 1, levels), F32),
        in_specs=[vmem],
        out_specs=vmem,
        scratch_shapes=[
            pltpu.VMEM((n_pencil, 8, lanes), F32),
            pltpu.VMEM((8, lanes), F32),
            pltpu.VMEM((n_slab, 8, lanes), F32),
            dma, dma, dma, dma,
        ],
        compiler_params=pltpu.CompilerParams(collective_id=1, has_side_effects=True, vmem_limit_bytes=24 << 20),
        name="far",
    )(moment)
    return vorticity_out, far_velocity


def solution(mesh):
    in_specs = (
        P(None, "slab", "pencil", None),
        P(None, "slab", "pencil", None),
        P("slab", "pencil", None),
        P(("slab", "pencil"), None, None),
        P(("slab", "pencil"), None),
        P(("slab", "pencil"), None),
        P(("slab", "pencil")),
    )
    out_specs = (P(None, "slab", "pencil", None), P(None, "slab", "pencil", None))
    step = functools.partial(per_device, mesh.shape["slab"], mesh.shape["pencil"])
    return jax.shard_map(step, mesh=mesh, in_specs=in_specs, out_specs=out_specs, check_vma=False)
```

time: 316 us -> 62.2 us (0.20)
  other arithmetic: 97.9 us -> 0 us
  blocking collectives: 71.8 us -> 0 us
  local copies, waits for them, and re-layouts: 73.8 us -> 5.95 us
  Pallas kernels: 0 us -> 54.6 us
  waiting for transfers between devices: 40.6 us -> 0 us
  starting transfers between devices: 14 us -> 0 us
  between operations: 15.1 us -> 1.34 us
    all_gather x1 -> x0, blocking collectives: 71.8 us -> none  [per_device(): piece = lax.all_gather(moment, ('slab', 'pencil'), axis=1, tiled=True)]
    scatter-add x1 -> x0, other arithmetic: 70.1 us -> none  [deposit(): return field_flat.at[:, local_cells.reshape(-1)].add(values)]
    pallas_call x0 -> x3, Pallas kernels: none -> 54.6 us  [the longest x1 19.4 us: per_device(): pl.pallas_call(functools.partial(exchange_kernel, n_slab, n_pencil), out_...]
    all_gather x1 -> x0, waiting for transfers between devices: 37.4 us -> none  [per_device(): arrived = lax.all_gather(payload, 'slab', axis=0, tiled=True)]
    scatter x1 -> x0, local copies, waits for them, and re-layouts: 29.2 us -> none  [per_device(): compact_weights = jnp.zeros((rows_kept, 3, tile_len), jnp.float32).at[pos...]
    add x1 -> x0, local copies, waits for them, and re-layouts: 16.6 us -> none  [advance(): return own_vort + time_step * (stretch + diffuse)]
    unnamed x12 -> x19, local copies, waits for them, and re-layouts: 21.1 us -> 5.95 us
    ppermute x4 -> x0, starting transfers between devices: 14 us -> none  [the longest x2 7 us: with_halo(): before = lax.ppermute(last, axis, up)]
  transfers between devices with their start and end apart: 5 -> 0, of which waited for: 5 -> 0; matrix products, arithmetic and copies ran while one was open for 7% -> 0% of each run, Pallas kernels for 0% -> 0%
where the time goes in v1:
time: 62.2 us; the launch traced here: 61.9 us
  Pallas kernels  54.6 us (88%)
  local copies, waits for them, and re-layouts  5.95 us (10%)
  between operations  1.34 us (2%)
    pallas_call x1, Pallas kernels, per_device(): pl.pallas_call(functools.partial(exchange_kernel, n_slab, n_pencil), out_...  19.4 us
    pallas_call x1, Pallas kernels, per_device(): pl.pallas_call(functools.partial(far_kernel, n_slab, n_pencil, cx, cy, fl...  18.9 us
    pallas_call x1, Pallas kernels, per_device(): pl.pallas_call(functools.partial(block_kernel, n_slab, n_pencil), out_sha...  16.3 us
    unnamed x19, local copies, waits for them, and re-layouts  5.95 us

profile of v1, /device:TPU:1, one launch (start us, length us, event | category | flops | bytes accessed | tf_op | source)
XLA Modules:
  0.0 61.9 jit_solution(4611113819478937181)
XLA Ops:
  1.3 0.0 copy-start.8
  1.3 0.6 %copy-done.8 = s32[32,1]{0,1:T(1,128)S(1)} copy-done((s32[32,1]{0,1:T(1,128)S(1)}, s32[32,1]{0,1:T(1,128)}, u32[]{:S(2)}) %copy-start.8) | copy-done | bytes 152
  1.9 0.0 copy-start
  1.9 1.1 %copy-done = f32[3,8,32,256]{3,2,1,0:T(8,128)S(1)} copy-done((f32[3,8,32,256]{3,2,1,0:T(8,128)S(1)}, f32[3,8,32,256]{3,2,1,0:T(8,128)}, u32[]{:S(2)}) %copy-start) | copy-done | bytes 786456
  3.1 0.0 copy-start.2
  3.1 1.1 %copy-done.2 = f32[3,8,32,256]{3,2,1,0:T(8,128)S(1)} copy-done((f32[3,8,32,256]{3,2,1,0:T(8,128)S(1)}, f32[3,8,32,256]{3,2,1,0:T(8,128)}, u32[]{:S(2)}) %copy-start.2) | copy-done | bytes 786456
  4.2 0.0 copy-start.4
  4.2 0.9 %copy-done.4 = f32[8,32,256]{2,1,0:T(8,128)S(1)} copy-done((f32[8,32,256]{2,1,0:T(8,128)S(1)}, f32[8,32,256]{2,1,0:T(8,128)}, u32[]{:S(2)}) %copy-start.4) | copy-done | bytes 262168
  5.2 0.0 copy-start.6
  5.2 0.8 %copy-done.6 = f32[32,3,128]{2,0,1:T(8,128)S(1)} copy-done((f32[32,3,128]{2,0,1:T(8,128)S(1)}, f32[32,3,128]{2,0,1:T(8,128)}, u32[]{:S(2)}) %copy-start.6) | copy-done | bytes 49176
  6.0 0.0 copy-start.7
  6.0 0.7 %copy-done.7 = s32[32,128]{1,0:T(8,128)S(1)} copy-done((s32[32,128]{1,0:T(8,128)S(1)}, s32[32,128]{1,0:T(8,128)}, u32[]{:S(2)}) %copy-start.7) | copy-done | bytes 16408
  6.7 0.0 copy-start.1
  6.7 0.0 copy-start.3
  6.7 0.0 copy-start.5
  6.7 19.4 %exchange.1 = (f32[32,8,128]{2,1,0:T(8,128)S(1)}, f32[2,7,32,256]{3,2,1,0:T(8,128)S(1)}, f32[2,7,8,256]{3,2,1,0:T(8,128)S(1)}) custom-call(f32[3,8,32,256]{3,2,1,0:T(8,128)S(1)} %copy-done, f32[3,8,32,256]{3,2,1,0:T(8,128)S(1)} %copy-done.2, f32[8,32,256]{2,1,0:T(8,128)S(1)} %copy-done.4, f32[3,32,128]{2,1,0:T(8,128)S(1)} %bitcast.2, ...), custom_call_target="tpu_custom_call" | custom-call | tf_op jit(solution)/shard_map/exchange/pallas_call | solution.py:263
  26.0 0.0 copy-done.1
  26.1 0.0 copy-done.3
  26.1 0.0 copy-done.5
  26.1 16.3 %block.1 = (f32[3,8,32,256]{3,2,1,0:T(8,128)}, f32[8,128]{1,0:T(8,128)S(1)}) custom-call(f32[3,8,32,256]{3,2,1,0:T(8,128)S(1)} %copy-done.1, f32[3,8,32,256]{3,2,1,0:T(8,128)S(1)} %copy-done.3, f32[8,32,256]{2,1,0:T(8,128)S(1)} %copy-done.5, f32[2,7,32,256]{3,2,1,0:T(8,128)S(1)} %get-tuple-element.7.xhalo, f32[2,7,8,256]{3,2,1,0:T(8,128)S(1)} %get-tuple-element.8.yhalo, ...), custom_call_target="tpu_custom_call" | custom-call | tf_op jit(solution)/shard_map/block/pallas_call | solution.py:281
  42.4 18.9 %far.1 = f32[3,1,1,16]{3,2,1,0:T(1,128)S(1)} custom-call(f32[8,128]{1,0:T(8,128)S(1)} %get-tuple-element.11.moment), custom_call_target="tpu_custom_call" | custom-call | tf_op jit(solution)/shard_map/far/pallas_call | solution.py:299
  61.3 0.6 copy.11
Async XLA Ops:
  1.3 0.7 %copy-start.8 = (s32[32,1]{0,1:T(1,128)S(1)}, s32[32,1]{0,1:T(1,128)}, u32[]{:S(2)}) copy-start(s32[32,1]{0,1:T(1,128)} %param.12) | copy-start | bytes 388
  1.9 1.1 %copy-start = (f32[3,8,32,256]{3,2,1,0:T(8,128)S(1)}, f32[3,8,32,256]{3,2,1,0:T(8,128)}, u32[]{:S(2)}) copy-start(f32[3,8,32,256]{3,2,1,0:T(8,128)} %vort.3) | copy-start | bytes 2359300
  3.1 1.1 %copy-start.2 = (f32[3,8,32,256]{3,2,1,0:T(8,128)S(1)}, f32[3,8,32,256]{3,2,1,0:T(8,128)}, u32[]{:S(2)}) copy-start(f32[3,8,32,256]{3,2,1,0:T(8,128)} %velo.3) | copy-start | bytes 2359300
  4.2 0.9 %copy-start.4 = (f32[8,32,256]{2,1,0:T(8,128)S(1)}, f32[8,32,256]{2,1,0:T(8,128)}, u32[]{:S(2)}) copy-start(f32[8,32,256]{2,1,0:T(8,128)} %visc.3) | copy-start | bytes 786436
  5.2 0.8 %copy-start.6 = (f32[32,3,128]{2,0,1:T(8,128)S(1)}, f32[32,3,128]{2,0,1:T(8,128)}, u32[]{:S(2)}) copy-start(f32[32,3,128]{2,0,1:T(8,128)} %param.10) | copy-start | bytes 147460
  6.0 0.7 %copy-start.7 = (s32[32,128]{1,0:T(8,128)S(1)}, s32[32,128]{1,0:T(8,128)}, u32[]{:S(2)}) copy-start(s32[32,128]{1,0:T(8,128)} %cells.1) | copy-start | bytes 49156
  6.7 19.4 %copy-start.1 = (f32[3,8,32,256]{3,2,1,0:T(8,128)S(1)}, f32[3,8,32,256]{3,2,1,0:T(8,128)}, u32[]{:S(2)}) copy-start(f32[3,8,32,256]{3,2,1,0:T(8,128)} %vort.3) | copy-start | bytes 2359300
  6.7 19.4 %copy-start.3 = (f32[3,8,32,256]{3,2,1,0:T(8,128)S(1)}, f32[3,8,32,256]{3,2,1,0:T(8,128)}, u32[]{:S(2)}) copy-start(f32[3,8,32,256]{3,2,1,0:T(8,128)} %velo.3) | copy-start | bytes 2359300
  6.7 19.4 %copy-start.5 = (f32[8,32,256]{2,1,0:T(8,128)S(1)}, f32[8,32,256]{2,1,0:T(8,128)}, u32[]{:S(2)}) copy-start(f32[8,32,256]{2,1,0:T(8,128)} %visc.3) | copy-start | bytes 786436

commit v2 on v1

v2 whole, which is shorter than its diff:
```python
import functools

import jax
import jax.numpy as jnp
from jax import lax
from jax.experimental import pallas as pl
from jax.experimental.pallas import tpu as pltpu
from jax.sharding import PartitionSpec as P

CB = 16
FIELDS = 7
time_step = 0.1
VMEM_LIMIT = 60 << 20
HIGH = lax.Precision.HIGHEST
F32 = jnp.float32
BF16 = jnp.bfloat16
MESH = pl.DeviceIdType.MESH


def iota(shape, dim):
    return lax.broadcasted_iota(jnp.int32, shape, dim)


def signal_peers(axis, me, count, offsets):
    barrier = pltpu.get_barrier_semaphore()

    def one(k, carry):
        peer = lax.rem(me + k, count)
        pl.semaphore_signal(barrier, inc=1, device_id={axis: peer}, device_id_type=MESH)
        return carry

    lax.fori_loop(offsets[0], offsets[1], one, 0)


def remote(src, dst, send_sem, recv_sem, device):
    return pltpu.make_async_remote_copy(
        src_ref=src, dst_ref=dst, send_sem=send_sem, recv_sem=recv_sem, device_id=device, device_id_type=MESH
    )


def pack_tiles(weights, cells, dest, live, send, n_slab):
    tiles = cells.shape[0]
    slab = iota((n_slab, tiles), 0)
    tile = iota((n_slab, tiles), 1)
    match = jnp.where((dest[...] == slab) & (tile < live), 1.0, 0.0)
    earlier = jnp.where(iota((tiles, tiles), 0) < iota((tiles, tiles), 1), 1.0, 0.0)
    before = jnp.dot(match, earlier, preferred_element_type=F32)
    for j in range(2):
        pick = jnp.where(before == j, match, 0.0)
        for c in range(4):
            rows = weights[c] if c < 3 else (cells[...] + 1).astype(F32)
            send[:, 4 * j + c, :] = jnp.dot(pick, rows, precision=HIGH, preferred_element_type=F32)


def deposit(tiles, lhs, rhs, total, first, last):
    rows, nz = total.shape[0] // 3, total.shape[1]
    width = 2 * tiles.shape[2]
    group = lhs.shape[1] // (2 * width)
    shift = nz.bit_length() - 1
    number = iota((rows, width), 0).astype(F32).astype(BF16)
    one, zero = jnp.ones((), BF16), jnp.zeros((), BF16)

    def add(i, carry):
        for g in range(group):
            tile = tiles[i * group + g]
            entry = [jnp.concatenate([tile[c : c + 1], tile[4 + c : 5 + c]], axis=1) for c in range(4)]
            cell = entry[3].astype(jnp.int32) - 1
            high = (cell >> shift).astype(F32).astype(BF16)
            low = (cell & (nz - 1)).astype(F32).astype(BF16)
            here = number == high
            at = 2 * g * width
            for c in range(3):
                first_piece = entry[c].astype(BF16)
                second_piece = (entry[c] - first_piece.astype(F32)).astype(BF16)
                lhs[c * rows : (c + 1) * rows, at : at + width] = jnp.where(here, first_piece, zero)
                lhs[c * rows : (c + 1) * rows, at + width : at + 2 * width] = jnp.where(here, second_piece, zero)
            onehot = jnp.where(number == low, one, zero)
            rhs[:, at : at + width] = onehot
            rhs[:, at + width : at + 2 * width] = onehot
        total[...] += lax.dot_general(lhs[...], rhs[...], (((1,), (1,)), ((), ())), preferred_element_type=F32)
        return carry

    lax.fori_loop(first, last, add, 0)


def tile_moments(tiles, nz, base, lanes):
    levels = nz // CB
    sums = [[None] * levels for c in range(3)]
    for j in range(2):
        code = tiles[:, 4 * j + 3, :].astype(jnp.int32) - 1
        level = (code & (nz - 1)) // CB
        for l in range(levels):
            here = level == l
            for c in range(3):
                part = jnp.where(here, tiles[:, 4 * j + c, :], 0.0)
                part = jnp.sum(part.reshape(part.shape[0] // 8, 8, part.shape[1]), axis=0)
                sums[c][l] = part if j == 0 else sums[c][l] + part
    place = jnp.where(iota((8 * levels, lanes), 0) // 8 + base == iota((8 * levels, lanes), 1), 1.0, 0.0)
    ones = jnp.ones((8, tiles.shape[2]), F32)
    rows = []
    for c in range(3):
        stacked = jnp.concatenate(sums[c], axis=0)
        line = lax.dot_general(ones, stacked, (((1,), (1,)), ((), ())), precision=HIGH, preferred_element_type=F32)
        rows.append(jnp.dot(line, place, precision=HIGH, preferred_element_type=F32)[0:1])
    return jnp.concatenate(rows + [jnp.zeros((5, lanes), F32)], axis=0)


def step_kernel(
    n_slab, n_pencil, sigma, vort, velo, visc, weights, cells, dest, count,
    out, far,
    field, wtile, ctile, send, tiles, yface, yhalo, lhs, rhs, total, moment, inbox, slab_moment, everywhere,
    load_sem, xsend, xrecv, ysend, yrecv, tsend, trecv, asend, arecv, bsend, brecv,
):
    slab, pencil = lax.axis_index("slab"), lax.axis_index("pencil")
    cx, cy, nz = out.shape[1], out.shape[2], out.shape[3]
    lanes = moment.shape[1]
    levels = nz // CB
    tile_loads = [
        pltpu.make_async_copy(weights, wtile, load_sem.at[3]),
        pltpu.make_async_copy(cells, ctile, load_sem.at[4]),
    ]
    loads = [
        pltpu.make_async_copy(vort, field.at[0:3, 1 : cx + 1], load_sem.at[0]),
        pltpu.make_async_copy(velo, field.at[3:6, 1 : cx + 1], load_sem.at[1]),
        pltpu.make_async_copy(visc, field.at[6, 1 : cx + 1], load_sem.at[2]),
    ]
    for load in tile_loads + loads:
        load.start()
    barrier = pltpu.get_barrier_semaphore()
    signal_peers("slab", slab, n_slab, (1, n_slab))
    signal_peers("pencil", pencil, n_pencil, (1, n_pencil))
    for load in tile_loads:
        load.wait()
    pack_tiles(wtile, ctile, dest, count[0], send, n_slab)
    total[...] = jnp.zeros_like(total)
    for load in loads:
        load.wait()
    for c in range(FIELDS):
        yface[0, c] = field[c, 1 : cx + 1, 0, :]
        yface[1, c] = field[c, 1 : cx + 1, cy - 1, :]
    pl.semaphore_wait(barrier, n_slab - 1 + n_pencil - 1)

    s_up, s_down = lax.rem(slab + 1, n_slab), lax.rem(slab + n_slab - 1, n_slab)
    p_up, p_down = lax.rem(pencil + 1, n_pencil), lax.rem(pencil + n_pencil - 1, n_pencil)
    yhalos = [
        remote(yface.at[0], yhalo.at[1], ysend.at[0], yrecv.at[1], {"pencil": p_down}),
        remote(yface.at[1], yhalo.at[0], ysend.at[1], yrecv.at[0], {"pencil": p_up}),
    ]
    xhalos = [
        remote(field.at[:, 1], field.at[:, cx + 1], xsend.at[0], xrecv.at[1], {"slab": s_down}),
        remote(field.at[:, cx], field.at[:, 0], xsend.at[1], xrecv.at[0], {"slab": s_up}),
    ]
    for halo in yhalos + xhalos:
        halo.start()

    def deliver(k, carry):
        peer = lax.rem(slab + k, n_slab)
        remote(send.at[peer], tiles.at[k], tsend, trecv, {"slab": peer}).start()
        return carry

    lax.fori_loop(1, n_slab, deliver, 0)
    tiles[0] = send[slab]
    delivered = remote(send.at[1:n_slab], tiles.at[1:n_slab], tsend, trecv, {"slab": s_up})
    for halo in yhalos:
        halo.wait()

    row = iota((cy, nz), 0)
    first_row, last_row = row == 0, row == cy - 1
    has_before, has_after = pencil > 0, pencil < n_pencil - 1

    def plane(x, sums):
        def ahead_y(c):
            edge = jnp.where(has_after, yhalo[1, c, pl.ds(x, 1), :], 0.0)
            return jnp.where(last_row, edge, pltpu.roll(field[c, x + 1], cy - 1, 0))

        def behind_y(c):
            edge = jnp.where(has_before, yhalo[0, c, pl.ds(x, 1), :], 0.0)
            return jnp.where(first_row, edge, pltpu.roll(field[c, x + 1], 1, 0))

        neighbours = [
            (lambda c: field[c, x + 2], lambda c: field[c, x]),
            (ahead_y, behind_y),
            (lambda c: pltpu.roll(field[c, x + 1], nz - 1, 1), lambda c: pltpu.roll(field[c, x + 1], 1, 1)),
        ]
        own = [field[c, x + 1] for c in range(3)]
        own_visc = field[6, x + 1]
        change = [jnp.zeros_like(own_visc) for c in range(3)]
        for d, (forward, backward) in enumerate(neighbours):
            factor = 0.5 * own[d]
            face_ahead = 0.5 * (own_visc + forward(6))
            face_behind = 0.5 * (own_visc + backward(6))
            for c in range(3):
                change[c] += factor * (forward(3 + c) - backward(3 + c))
                change[c] += face_ahead * (forward(c) - own[c])
                change[c] += face_behind * (backward(c) - own[c])
        result = []
        for c in range(3):
            value = own[c] + time_step * change[c]
            out[c, x] = value
            result.append(sums[c] + jnp.sum(value, axis=0, keepdims=True))
        return tuple(result)

    sums = lax.fori_loop(1, cx - 1, plane, tuple(jnp.zeros((1, nz), F32) for c in range(3)))
    for halo in xhalos:
        halo.wait()
    field[:, 0] = jnp.where(slab > 0, field[:, 0], 0.0)
    field[:, cx + 1] = jnp.where(slab < n_slab - 1, field[:, cx + 1], 0.0)
    sums = lax.fori_loop(0, 2, lambda i, sums: plane(i * (cx - 1), sums), sums)
    delivered.wait_recv()
    group = jnp.where(iota((nz, lanes), 0) // CB + pencil * levels == iota((nz, lanes), 1), 1.0, 0.0)
    stacked = jnp.concatenate(list(sums) + [jnp.zeros((5, nz), F32)], axis=0)
    moment[...] = jnp.dot(stacked, group, precision=HIGH, preferred_element_type=F32) + tile_moments(
        tiles, nz, pencil * levels, lanes
    )

    def to_pencil(k, carry):
        remote(moment, inbox.at[k], asend, arecv, {"pencil": lax.rem(pencil + k, n_pencil)}).start()
        return carry

    lax.fori_loop(1, n_pencil, to_pencil, 0)
    inbox[0] = moment[...]
    arrived = remote(inbox.at[1:n_pencil], inbox.at[1:n_pencil], asend, arecv, {"pencil": p_up})
    groups = tiles.shape[0] * 4 * tiles.shape[2] // lhs.shape[1]
    deposit(tiles, lhs, rhs, total, 0, groups * 3 // 8)
    arrived.wait_recv()
    slab_moment[...] = jnp.sum(inbox[...], axis=0)

    def to_slab(k, carry):
        peer = lax.rem(slab + k, n_slab)
        remote(slab_moment, everywhere.at[slab], bsend, brecv, {"slab": peer}).start()
        return carry

    lax.fori_loop(1, n_slab, to_slab, 0)
    everywhere[slab] = slab_moment[...]
    gathered = remote(everywhere.at[1:n_slab], everywhere.at[1:n_slab], bsend, brecv, {"slab": s_up})
    deposit(tiles, lhs, rhs, total, groups * 3 // 8, groups)
    for c in range(3):
        out[c] += total[c * cx * cy : (c + 1) * cx * cy].reshape(cx, cy, nz)
    gathered.wait_recv()
    delivered.wait_send()
    arrived.wait_send()
    gathered.wait_send()

    shape = (n_slab, lanes)
    rel_x = ((slab - iota(shape, 0)) * cx).astype(F32)
    rel_y = ((pencil - iota(shape, 1) // levels) * cy).astype(F32)
    level = iota(shape, 1) % levels
    plane_sq = rel_x * rel_x + rel_y * rel_y + sigma * sigma
    m0, m1, m2 = (everywhere[:, c, :] for c in range(3))
    fixed = (-(rel_y * m2), rel_x * m2, rel_y * m0 - rel_x * m1)
    far_sums = ([], [], [])
    for target in range(levels):
        rel_z = ((target - level) * CB).astype(F32)
        inverse = lax.rsqrt(plane_sq + rel_z * rel_z)
        weight = inverse * inverse * inverse
        terms = (rel_z * m1 + fixed[0], fixed[1] - rel_z * m0, fixed[2])
        for c in range(3):
            far_sums[c].append(jnp.sum(weight * terms[c], axis=0, keepdims=True))
    ones = jnp.ones((8, lanes), F32)
    for c in range(3):
        rows = jnp.concatenate(far_sums[c], axis=0)
        far[c, 0] = lax.dot_general(ones, rows, (((1,), (1,)), ((), ())), precision=HIGH, preferred_element_type=F32)[0:1]


GROUP = 4


def per_device(n_slab, n_pencil, vorticity, velocity, viscosity, tile_weights, tile_cells, tile_dest, tile_count):
    _, cx, cy, nz = vorticity.shape
    n_tiles, tile_len = tile_cells.shape
    levels = nz // CB
    lanes = n_pencil * levels
    hbm = pl.BlockSpec(memory_space=pltpu.HBM)
    vmem = pl.BlockSpec(memory_space=pltpu.VMEM)
    smem = pl.BlockSpec(memory_space=pltpu.SMEM)
    dma = pltpu.SemaphoreType.DMA
    return pl.pallas_call(
        functools.partial(step_kernel, n_slab, n_pencil, float(cx * n_slab // 4)),
        out_shape=(jax.ShapeDtypeStruct(vorticity.shape, F32), jax.ShapeDtypeStruct((3, 1, 1, levels), F32)),
        in_specs=[hbm, hbm, hbm, hbm, hbm, vmem, smem],
        out_specs=(vmem, vmem),
        scratch_shapes=[
            pltpu.VMEM((FIELDS, cx + 2, cy, nz), F32),
            pltpu.VMEM((3, n_tiles, tile_len), F32),
            pltpu.VMEM((n_tiles, tile_len), jnp.int32),
            pltpu.VMEM((n_slab, 8, tile_len), F32),
            pltpu.VMEM((n_slab, 8, tile_len), F32),
            pltpu.VMEM((2, FIELDS, cx, nz), F32),
            pltpu.VMEM((2, FIELDS, cx, nz), F32),
            pltpu.VMEM((3 * cx * cy, GROUP * 4 * tile_len), BF16),
            pltpu.VMEM((nz, GROUP * 4 * tile_len), BF16),
            pltpu.VMEM((3 * cx * cy, nz), F32),
            pltpu.VMEM((8, lanes), F32),
            pltpu.VMEM((n_pencil, 8, lanes), F32),
            pltpu.VMEM((8, lanes), F32),
            pltpu.VMEM((n_slab, 8, lanes), F32),
            dma((5,)), dma((2,)), dma((2,)), dma((2,)), dma((2,)), dma, dma, dma, dma, dma, dma,
        ],
        compiler_params=pltpu.CompilerParams(collective_id=0, has_side_effects=True, vmem_limit_bytes=VMEM_LIMIT),
        name="step",
    )(
        vorticity, velocity, viscosity, jnp.transpose(tile_weights, (1, 0, 2)), tile_cells,
        tile_dest.reshape(1, -1), tile_count,
    )


def solution(mesh):
    in_specs = (
        P(None, "slab", "pencil", None),
        P(None, "slab", "pencil", None),
        P("slab", "pencil", None),
        P(("slab", "pencil"), None, None),
        P(("slab", "pencil"), None),
        P(("slab", "pencil"), None),
        P(("slab", "pencil")),
    )
    out_specs = (P(None, "slab", "pencil", None), P(None, "slab", "pencil", None))
    step = functools.partial(per_device, mesh.shape["slab"], mesh.shape["pencil"])
    return jax.shard_map(step, mesh=mesh, in_specs=in_specs, out_specs=out_specs, check_vma=False)
```

time: 62.2 us -> 44.3 us (0.71)
  Pallas kernels: 54.6 us -> 40.2 us
  local copies, waits for them, and re-layouts: 5.95 us -> 2.66 us
    pallas_call x3 -> x1, Pallas kernels: 54.6 us -> 40.2 us  [per_device(): pl.pallas_call(functools.partial(step_kernel, n_slab, n_pencil, float(cx...]
    unnamed x19 -> x4, local copies, waits for them, and re-layouts: 5.95 us -> 2.66 us
where the time goes in v2:
time: 44.3 us; the launch traced here: 44.2 us
  Pallas kernels  40.2 us (91%)
  local copies, waits for them, and re-layouts  2.66 us (6%)
  between operations  1.3 us (3%)
    pallas_call x1, Pallas kernels, per_device(): pl.pallas_call(functools.partial(step_kernel, n_slab, n_pencil, float(cx...  40.2 us
    unnamed x4, local copies, waits for them, and re-layouts  2.66 us

profile of v2, /device:TPU:1, one launch (start us, length us, event | category | flops | bytes accessed | tf_op | source)
XLA Modules:
  0.0 44.2 jit_solution(10840361199073711942)
XLA Ops:
  1.3 40.2 %step.1 = (f32[3,8,32,256]{3,2,1,0:T(8,128)}, f32[3,1,1,16]{3,2,1,0:T(1,128)}) custom-call(f32[3,8,32,256]{3,2,1,0:T(8,128)} %vort.1, f32[3,8,32,256]{3,2,1,0:T(8,128)} %velo.1, f32[8,32,256]{2,1,0:T(8,128)} %visc.1, f32[3,32,128]{2,1,0:T(8,128)} %bitcast.2, s32[32,128]{1,0:T(8,128)} %cells.1, s32[1,32]{1,0:T(1,128)} %bitcast.3, s32[1]{0:T(128)S(6)} %copy.11.count), custom_call_target="tpu_custom_call" | custom-call | tf_op jit(solution)/shard_map/step/pallas_call | solution.py:277
  41.5 0.0 copy-start
  41.5 2.1 %copy.12 = f32[3,8,32,256]{3,2,1,0:T(8,128)} copy(f32[3,8,32,256]{3,2,1,0:T(8,128)} %get-tuple-element.4) | data formatting | bytes 1572864
  43.6 0.0 copy-done
  43.6 0.6 %copy.13 = f32[3,1,1,16]{3,2,1,0:T(1,128)} copy(f32[3,1,1,16]{3,2,1,0:T(1,128)S(1)} %copy-done) | data formatting | bytes 384
Async XLA Ops:
  41.5 2.1 %copy-start = (f32[3,1,1,16]{3,2,1,0:T(1,128)S(1)}, f32[3,1,1,16]{3,2,1,0:T(1,128)}, u32[]{:S(2)}) copy-start(f32[3,1,1,16]{3,2,1,0:T(1,128)} %get-tuple-element.5) | copy-start | bytes 580

commit v3 on v2

--- a/solution.py
+++ b/solution.py
@@ -21,15 +21,16 @@
     return lax.broadcasted_iota(jnp.int32, shape, dim)
 
 
-def signal_peers(axis, me, count, offsets):
-    barrier = pltpu.get_barrier_semaphore()
-
-    def one(k, carry):
-        peer = lax.rem(me + k, count)
-        pl.semaphore_signal(barrier, inc=1, device_id={axis: peer}, device_id_type=MESH)
+def offset(i):
+    return (2 * (i % 2) - 1) * ((i + 1) // 2)
+
+
+def far_first(first, last, one):
+    def body(j, carry):
+        one(last - j)
         return carry
 
-    lax.fori_loop(offsets[0], offsets[1], one, 0)
+    lax.fori_loop(0, last - first + 1, body, 0)
 
 
 def remote(src, dst, send_sem, recv_sem, device):
@@ -38,8 +39,9 @@
     )
 
 
-def pack_tiles(weights, cells, dest, live, send, n_slab):
-    tiles = cells.shape[0]
+def pack_tiles(weights, cells, dest, live, send, sums, nz):
+    n_slab = send.shape[0]
+    tiles, lanes = cells.shape
     slab = iota((n_slab, tiles), 0)
     tile = iota((n_slab, tiles), 1)
     match = jnp.where((dest[...] == slab) & (tile < live), 1.0, 0.0)
@@ -50,6 +52,16 @@
         for c in range(4):
             rows = weights[c] if c < 3 else (cells[...] + 1).astype(F32)
             send[:, 4 * j + c, :] = jnp.dot(pick, rows, precision=HIGH, preferred_element_type=F32)
+    levels = nz // CB
+    level = (cells[...] & (nz - 1)) // CB
+    lane = iota((tiles, lanes), 1)
+    by_level = jnp.zeros((tiles, lanes), F32)
+    for l in range(levels):
+        here = level == l
+        for c in range(3):
+            total = jnp.sum(jnp.where(here, weights[c], 0.0), axis=1, keepdims=True)
+            by_level = jnp.where(lane == c * levels + l, total, by_level)
+    sums[:, 0, :] = jnp.dot(match, by_level, precision=HIGH, preferred_element_type=F32)
 
 
 def deposit(tiles, lhs, rhs, total, first, last):
@@ -83,84 +95,101 @@
     lax.fori_loop(first, last, add, 0)
 
 
-def tile_moments(tiles, nz, base, lanes):
-    levels = nz // CB
-    sums = [[None] * levels for c in range(3)]
-    for j in range(2):
-        code = tiles[:, 4 * j + 3, :].astype(jnp.int32) - 1
-        level = (code & (nz - 1)) // CB
-        for l in range(levels):
-            here = level == l
-            for c in range(3):
-                part = jnp.where(here, tiles[:, 4 * j + c, :], 0.0)
-                part = jnp.sum(part.reshape(part.shape[0] // 8, 8, part.shape[1]), axis=0)
-                sums[c][l] = part if j == 0 else sums[c][l] + part
-    place = jnp.where(iota((8 * levels, lanes), 0) // 8 + base == iota((8 * levels, lanes), 1), 1.0, 0.0)
-    ones = jnp.ones((8, tiles.shape[2]), F32)
-    rows = []
-    for c in range(3):
-        stacked = jnp.concatenate(sums[c], axis=0)
-        line = lax.dot_general(ones, stacked, (((1,), (1,)), ((), ())), precision=HIGH, preferred_element_type=F32)
-        rows.append(jnp.dot(line, place, precision=HIGH, preferred_element_type=F32)[0:1])
-    return jnp.concatenate(rows + [jnp.zeros((5, lanes), F32)], axis=0)
-
-
 def step_kernel(
     n_slab, n_pencil, sigma, vort, velo, visc, weights, cells, dest, count,
-    out, far,
-    field, wtile, ctile, send, tiles, yface, yhalo, lhs, rhs, total, moment, inbox, slab_moment, everywhere,
-    load_sem, xsend, xrecv, ysend, yrecv, tsend, trecv, asend, arecv, bsend, brecv,
+    out_hbm, far,
+    field, wtile, ctile, send, tiles, sums_send, sums_in, yface, yhalo, lhs, rhs, total, out, moment, inbox, slab_moment,
+    everywhere, load_sem, xsend, xrecv, ysend, yrecv, tsend, trecv, msend, mrecv, asend, arecv, bsend, brecv, ready, out_sem,
 ):
     slab, pencil = lax.axis_index("slab"), lax.axis_index("pencil")
     cx, cy, nz = out.shape[1], out.shape[2], out.shape[3]
     lanes = moment.shape[1]
     levels = nz // CB
-    tile_loads = [
-        pltpu.make_async_copy(weights, wtile, load_sem.at[3]),
-        pltpu.make_async_copy(cells, ctile, load_sem.at[4]),
-    ]
+    waves = [min(2 * NEAR, n_slab - 1)]
+    while waves[-1] < n_slab - 1:
+        waves.append(min(2 * waves[-1], n_slab - 1))
+
+    def slab_peer(i):
+        return {"slab": lax.rem(slab + offset(i) + n_slab, n_slab)}
+
+    def pencil_peer(i):
+        return {"pencil": lax.rem(pencil + offset(i) + n_pencil, n_pencil)}
+
     loads = [
         pltpu.make_async_copy(vort, field.at[0:3, 1 : cx + 1], load_sem.at[0]),
         pltpu.make_async_copy(velo, field.at[3:6, 1 : cx + 1], load_sem.at[1]),
         pltpu.make_async_copy(visc, field.at[6, 1 : cx + 1], load_sem.at[2]),
     ]
-    for load in tile_loads + loads:
+    tile_loads = [
+        pltpu.make_async_copy(weights, wtile, load_sem.at[3]),
+        pltpu.make_async_copy(cells, ctile, load_sem.at[4]),
+    ]
+    for load in loads + tile_loads:
         load.start()
     barrier = pltpu.get_barrier_semaphore()
-    signal_peers("slab", slab, n_slab, (1, n_slab))
-    signal_peers("pencil", pencil, n_pencil, (1, n_pencil))
-    for load in tile_loads:
-        load.wait()
-    pack_tiles(wtile, ctile, dest, count[0], send, n_slab)
-    total[...] = jnp.zeros_like(total)
+
+    def greet(where):
+        pl.semaphore_signal(barrier, inc=1, device_id=where, device_id_type=MESH)
+
+    far_first(1, waves[0], lambda i: greet(slab_peer(i)))
+    far_first(1, n_pencil - 1, lambda i: greet(pencil_peer(i)))
     for load in loads:
         load.wait()
     for c in range(FIELDS):
         yface[0, c] = field[c, 1 : cx + 1, 0, :]
         yface[1, c] = field[c, 1 : cx + 1, cy - 1, :]
-    pl.semaphore_wait(barrier, n_slab - 1 + n_pencil - 1)
-
-    s_up, s_down = lax.rem(slab + 1, n_slab), lax.rem(slab + n_slab - 1, n_slab)
-    p_up, p_down = lax.rem(pencil + 1, n_pencil), lax.rem(pencil + n_pencil - 1, n_pencil)
+    pl.semaphore_wait(barrier, waves[0] + n_pencil - 1)
+
+    s_up, s_down = slab_peer(1), slab_peer(2)
+    p_up, p_down = pencil_peer(1), pencil_peer(2)
     yhalos = [
-        remote(yface.at[0], yhalo.at[1], ysend.at[0], yrecv.at[1], {"pencil": p_down}),
-        remote(yface.at[1], yhalo.at[0], ysend.at[1], yrecv.at[0], {"pencil": p_up}),
+        remote(yface.at[0], yhalo.at[1], ysend.at[0], yrecv.at[1], p_down),
+        remote(yface.at[1], yhalo.at[0], ysend.at[1], yrecv.at[0], p_up),
     ]
     xhalos = [
-        remote(field.at[:, 1], field.at[:, cx + 1], xsend.at[0], xrecv.at[1], {"slab": s_down}),
-        remote(field.at[:, cx], field.at[:, 0], xsend.at[1], xrecv.at[0], {"slab": s_up}),
+        remote(field.at[:, 1], field.at[:, cx + 1], xsend.at[0], xrecv.at[1], s_down),
+        remote(field.at[:, cx], field.at[:, 0], xsend.at[1], xrecv.at[0], s_up),
     ]
     for halo in yhalos + xhalos:
         halo.start()
 
-    def deliver(k, carry):
-        peer = lax.rem(slab + k, n_slab)
-        remote(send.at[peer], tiles.at[k], tsend, trecv, {"slab": peer}).start()
-        return carry
-
-    lax.fori_loop(1, n_slab, deliver, 0)
+    def announce(step):
+        for i in (waves[step] - 1, waves[step]):
+            pl.semaphore_signal(ready.at[step], inc=1, device_id=slab_peer(i), device_id_type=MESH)
+
+    def destination(i):
+        return lax.rem(slab + offset(i) + n_slab, n_slab)
+
+    def send_sums(i):
+        remote(
+            sums_send.at[destination(i), 0:1], sums_in.at[i, 0:1], msend, mrecv, slab_peer(i)
+        ).start()
+
+    def send_tiles(wave):
+        first = 1 if wave == 0 else waves[wave - 1] + 1
+
+        def one(i):
+            remote(send.at[destination(i)], tiles.at[i], tsend.at[wave], trecv.at[wave], slab_peer(i)).start()
+
+        far_first(first, waves[wave], one)
+
+    def tiles_of(wave):
+        first = 1 if wave == 0 else waves[wave - 1] + 1
+        part = slice(first, waves[wave] + 1)
+        return remote(send.at[part], tiles.at[part], tsend.at[wave], trecv.at[wave], s_up)
+
+    if len(waves) > 1:
+        announce(0)
+    for load in tile_loads:
+        load.wait()
+    pack_tiles(wtile, ctile, dest, count[0], send, sums_send, nz)
     tiles[0] = send[slab]
-    delivered = remote(send.at[1:n_slab], tiles.at[1:n_slab], tsend, trecv, {"slab": s_up})
+    sums_in[0, 0:1] = sums_send[slab, 0:1]
+    total[...] = jnp.zeros_like(total)
+    if len(waves) > 1:
+        pl.semaphore_wait(ready.at[0], 2)
+    for step in range(1, len(waves) - 1):
+        announce(step)
     for halo in yhalos:
         halo.wait()
 
@@ -201,45 +230,53 @@
         return tuple(result)
 
     sums = lax.fori_loop(1, cx - 1, plane, tuple(jnp.zeros((1, nz), F32) for c in range(3)))
+    for step in range(1, len(waves) - 1):
+        pl.semaphore_wait(ready.at[step], 2)
+    far_first(1, n_slab - 1, send_sums)
+    for wave in range(len(waves)):
+        send_tiles(wave)
     for halo in xhalos:
         halo.wait()
     field[:, 0] = jnp.where(slab > 0, field[:, 0], 0.0)
     field[:, cx + 1] = jnp.where(slab < n_slab - 1, field[:, cx + 1], 0.0)
     sums = lax.fori_loop(0, 2, lambda i, sums: plane(i * (cx - 1), sums), sums)
-    delivered.wait_recv()
+    all_sums = remote(sums_send.at[1:n_slab, 0:1], sums_in.at[1:n_slab, 0:1], msend, mrecv, s_up)
+    all_sums.wait_recv()
+    line = jnp.sum(sums_in[:, 0, :], axis=0, keepdims=True)
+    width = sums_in.shape[2]
+    row, column = iota((8, width), 0), iota((8, width), 1)
+    tile_rows = jnp.where((column // levels == row) & (row < 3), line, 0.0)
+    place = jnp.where(iota((width, lanes), 0) % levels + pencil * levels == iota((width, lanes), 1), 1.0, 0.0)
     group = jnp.where(iota((nz, lanes), 0) // CB + pencil * levels == iota((nz, lanes), 1), 1.0, 0.0)
     stacked = jnp.concatenate(list(sums) + [jnp.zeros((5, nz), F32)], axis=0)
-    moment[...] = jnp.dot(stacked, group, precision=HIGH, preferred_element_type=F32) + tile_moments(
-        tiles, nz, pencil * levels, lanes
+    moment[...] = jnp.dot(
+        jnp.concatenate([stacked, tile_rows], axis=1), jnp.concatenate([group, place], axis=0),
+        precision=HIGH, preferred_element_type=F32,
     )
 
-    def to_pencil(k, carry):
-        remote(moment, inbox.at[k], asend, arecv, {"pencil": lax.rem(pencil + k, n_pencil)}).start()
-        return carry
-
-    lax.fori_loop(1, n_pencil, to_pencil, 0)
+    far_first(1, n_pencil - 1, lambda i: remote(moment, inbox.at[i], asend, arecv, pencil_peer(i)).start())
     inbox[0] = moment[...]
-    arrived = remote(inbox.at[1:n_pencil], inbox.at[1:n_pencil], asend, arecv, {"pencil": p_up})
+    arrived = remote(inbox.at[1:n_pencil], inbox.at[1:n_pencil], asend, arecv, p_up)
     groups = tiles.shape[0] * 4 * tiles.shape[2] // lhs.shape[1]
-    deposit(tiles, lhs, rhs, total, 0, groups * 3 // 8)
+    early = max(1, len(waves) - 1)
+    for wave in range(early):
+        tiles_of(wave).wait_recv()
+    deposit(tiles, lhs, rhs, total, 0, groups // 4)
     arrived.wait_recv()
     slab_moment[...] = jnp.sum(inbox[...], axis=0)
-
-    def to_slab(k, carry):
-        peer = lax.rem(slab + k, n_slab)
-        remote(slab_moment, everywhere.at[slab], bsend, brecv, {"slab": peer}).start()
-        return carry
-
-    lax.fori_loop(1, n_slab, to_slab, 0)
+    far_first(1, n_slab - 1, lambda i: remote(slab_moment, everywhere.at[slab], bsend, brecv, slab_peer(i)).start())
     everywhere[slab] = slab_moment[...]
-    gathered = remote(everywhere.at[1:n_slab], everywhere.at[1:n_slab], bsend, brecv, {"slab": s_up})
-    deposit(tiles, lhs, rhs, total, groups * 3 // 8, groups)
+    gathered = remote(everywhere.at[1:n_slab], everywhere.at[1:n_slab], bsend, brecv, s_up)
+    deposit(tiles, lhs, rhs, total, groups // 4, groups // 2)
+    for wave in range(early, len(waves)):
+        tiles_of(wave).wait_recv()
+    deposit(tiles, lhs, rhs, total, groups // 2, groups)
     for c in range(3):
         out[c] += total[c * cx * cy : (c + 1) * cx * cy].reshape(cx, cy, nz)
+    stores = [pltpu.make_async_copy(out.at[c], out_hbm.at[c], out_sem.at[c]) for c in range(3)]
+    for store in stores:
+        store.start()
     gathered.wait_recv()
-    delivered.wait_send()
-    arrived.wait_send()
-    gathered.wait_send()
 
     shape = (n_slab, lanes)
     rel_x = ((slab - iota(shape, 0)) * cx).astype(F32)
@@ -260,8 +297,25 @@
     for c in range(3):
         rows = jnp.concatenate(far_sums[c], axis=0)
         far[c, 0] = lax.dot_general(ones, rows, (((1,), (1,)), ((), ())), precision=HIGH, preferred_element_type=F32)[0:1]
-
-
+    all_sums.wait_send()
+    for wave in range(len(waves)):
+        tiles_of(wave).wait_send()
+    arrived.wait_send()
+    gathered.wait_send()
+    for store in stores:
+        store.wait()
+
+
+def hand_out_kernel(field, far, field_out, far_out, sem):
+    copies = [pltpu.make_async_copy(field.at[c], field_out.at[c], sem.at[c]) for c in range(3)]
+    for copy in copies:
+        copy.start()
+    far_out[...] = far[...]
+    for copy in copies:
+        copy.wait()
+
+
+NEAR = 4
 GROUP = 4
 
 
@@ -274,15 +328,18 @@
     vmem = pl.BlockSpec(memory_space=pltpu.VMEM)
     smem = pl.BlockSpec(memory_space=pltpu.SMEM)
     dma = pltpu.SemaphoreType.DMA
-    return pl.pallas_call(
+    outs = (jax.ShapeDtypeStruct(vorticity.shape, F32), jax.ShapeDtypeStruct((3, 1, 1, levels), F32))
+    field, far = pl.pallas_call(
         functools.partial(step_kernel, n_slab, n_pencil, float(cx * n_slab // 4)),
-        out_shape=(jax.ShapeDtypeStruct(vorticity.shape, F32), jax.ShapeDtypeStruct((3, 1, 1, levels), F32)),
+        out_shape=outs,
         in_specs=[hbm, hbm, hbm, hbm, hbm, vmem, smem],
-        out_specs=(vmem, vmem),
+        out_specs=(hbm, vmem),
         scratch_shapes=[
             pltpu.VMEM((FIELDS, cx + 2, cy, nz), F32),
             pltpu.VMEM((3, n_tiles, tile_len), F32),
             pltpu.VMEM((n_tiles, tile_len), jnp.int32),
+            pltpu.VMEM((n_slab, 8, tile_len), F32),
+            pltpu.VMEM((n_slab, 8, tile_len), F32),
             pltpu.VMEM((n_slab, 8, tile_len), F32),
             pltpu.VMEM((n_slab, 8, tile_len), F32),
             pltpu.VMEM((2, FIELDS, cx, nz), F32),
@@ -290,11 +347,13 @@
             pltpu.VMEM((3 * cx * cy, GROUP * 4 * tile_len), BF16),
             pltpu.VMEM((nz, GROUP * 4 * tile_len), BF16),
             pltpu.VMEM((3 * cx * cy, nz), F32),
+            pltpu.VMEM((3, cx, cy, nz), F32),
             pltpu.VMEM((8, lanes), F32),
             pltpu.VMEM((n_pencil, 8, lanes), F32),
             pltpu.VMEM((8, lanes), F32),
             pltpu.VMEM((n_slab, 8, lanes), F32),
-            dma((5,)), dma((2,)), dma((2,)), dma((2,)), dma((2,)), dma, dma, dma, dma, dma, dma,
+            dma((5,)), dma((2,)), dma((2,)), dma((2,)), dma((2,)), dma((4,)), dma((4,)), dma, dma, dma, dma, dma, dma,
+            pltpu.SemaphoreType.REGULAR((4,)), dma((3,)),
         ],
         compiler_params=pltpu.CompilerParams(collective_id=0, has_side_effects=True, vmem_limit_bytes=VMEM_LIMIT),
         name="step",
@@ -302,6 +361,15 @@
         vorticity, velocity, viscosity, jnp.transpose(tile_weights, (1, 0, 2)), tile_cells,
         tile_dest.reshape(1, -1), tile_count,
     )
+    return pl.pallas_call(
+        hand_out_kernel,
+        out_shape=outs,
+        in_specs=[hbm, vmem],
+        out_specs=(hbm, vmem),
+        scratch_shapes=[dma((3,))],
+        compiler_params=pltpu.CompilerParams(vmem_limit_bytes=VMEM_LIMIT),
+        name="hand_out",
+    )(field, far)
 
 
 def solution(mesh):

time: 44.3 us -> 60.5 us (1.37)
  Pallas kernels: 40.2 us -> 58.8 us
  local copies, waits for them, and re-layouts: 2.66 us -> 0 us
    pallas_call x0 -> x1, Pallas kernels: none -> 26.2 us  [per_device(): pl.pallas_call(hand_out_kernel, out_shape=outs, in_specs=[hbm, vmem], out...]
    pallas_call x1, Pallas kernels: 40.2 us -> 32.6 us  [per_device(): pl.pallas_call(functools.partial(step_kernel, n_slab, n_pencil, float(cx...]
    unnamed x4 -> x0, local copies, waits for them, and re-layouts: 2.66 us -> none
where the time goes in v3:
time: 60.5 us; the launch traced here: 60.1 us
  Pallas kernels  58.8 us (97%)
  between operations  1.29 us (2%)
    pallas_call x1, Pallas kernels, per_device(): pl.pallas_call(functools.partial(step_kernel, n_slab, n_pencil, float(cx...  32.6 us
    pallas_call x1, Pallas kernels, per_device(): pl.pallas_call(hand_out_kernel, out_shape=outs, in_specs=[hbm, vmem], out...  26.2 us

profile of v3, /device:TPU:1, one launch (start us, length us, event | category | flops | bytes accessed | tf_op | source)
XLA Modules:
  0.0 60.1 jit_solution(9122786538019192223)
XLA Ops:
  1.3 32.6 %step.1 = (f32[3,8,32,256]{3,2,1,0:T(8,128)}, f32[3,1,1,16]{3,2,1,0:T(1,128)}) custom-call(f32[3,8,32,256]{3,2,1,0:T(8,128)} %vort.1, f32[3,8,32,256]{3,2,1,0:T(8,128)} %velo.1, f32[8,32,256]{2,1,0:T(8,128)} %visc.1, f32[3,32,128]{2,1,0:T(8,128)} %bitcast.2, s32[32,128]{1,0:T(8,128)} %cells.1, s32[1,32]{1,0:T(1,128)} %bitcast.3, s32[1]{0:T(128)S(6)} %copy.9.count), custom_call_target="tpu_custom_call" | custom-call | tf_op jit(solution)/shard_map/step/pallas_call | solution.py:332
  33.9 26.2 %hand_out.1 = (f32[3,8,32,256]{3,2,1,0:T(8,128)}, f32[3,1,1,16]{3,2,1,0:T(1,128)}) custom-call(f32[3,8,32,256]{3,2,1,0:T(8,128)} %get-tuple-element.4.field, f32[3,1,1,16]{3,2,1,0:T(1,128)} %get-tuple-element.5.far), custom_call_target="tpu_custom_call" | custom-call | tf_op jit(solution)/shard_map/hand_out/pallas_call | solution.py:364

commit v4 on v3

--- a/solution.py
+++ b/solution.py
@@ -61,7 +61,11 @@
         for c in range(3):
             total = jnp.sum(jnp.where(here, weights[c], 0.0), axis=1, keepdims=True)
             by_level = jnp.where(lane == c * levels + l, total, by_level)
-    sums[:, 0, :] = jnp.dot(match, by_level, precision=HIGH, preferred_element_type=F32)
+    row = iota((NEAR * 8, tiles), 0)
+    member = jnp.where(row % 8 < n_slab // NEAR, row % 8 * NEAR + row // 8, -1)
+    match = jnp.where((dest[...] == member) & (iota((NEAR * 8, tiles), 1) < live), 1.0, 0.0)
+    added = jnp.dot(match, by_level, precision=HIGH, preferred_element_type=F32)
+    sums[...] = added.reshape(NEAR, 8, lanes)
 
 
 def deposit(tiles, lhs, rhs, total, first, last):
@@ -98,12 +102,12 @@
 def step_kernel(
     n_slab, n_pencil, sigma, vort, velo, visc, weights, cells, dest, count,
     out_hbm, far,
-    field, wtile, ctile, send, tiles, sums_send, sums_in, yface, yhalo, lhs, rhs, total, out, moment, inbox, slab_moment,
-    everywhere, load_sem, xsend, xrecv, ysend, yrecv, tsend, trecv, msend, mrecv, asend, arecv, bsend, brecv, ready, out_sem,
+    field, wtile, ctile, send, tiles, sums_send, sums_in, yface, yhalo, lhs, rhs, total, out, message, everywhere, kern,
+    partial, inbox, load_sem, xsend, xrecv, ysend, yrecv, tsend, trecv, msend, mrecv, asend, arecv, bsend, brecv, ready, out_sem,
 ):
     slab, pencil = lax.axis_index("slab"), lax.axis_index("pencil")
     cx, cy, nz = out.shape[1], out.shape[2], out.shape[3]
-    lanes = moment.shape[1]
+    lanes = partial.shape[1]
     levels = nz // CB
     waves = [min(2 * NEAR, n_slab - 1)]
     while waves[-1] < n_slab - 1:
@@ -160,11 +164,6 @@
     def destination(i):
         return lax.rem(slab + offset(i) + n_slab, n_slab)
 
-    def send_sums(i):
-        remote(
-            sums_send.at[destination(i), 0:1], sums_in.at[i, 0:1], msend, mrecv, slab_peer(i)
-        ).start()
-
     def send_tiles(wave):
         first = 1 if wave == 0 else waves[wave - 1] + 1
 
@@ -183,13 +182,24 @@
     for load in tile_loads:
         load.wait()
     pack_tiles(wtile, ctile, dest, count[0], send, sums_send, nz)
+    mine = lax.rem(slab, NEAR)
+
+    def to_member(j):
+        other = lax.rem(mine + j, NEAR)
+        return remote(sums_send.at[other], sums_in.at[j], msend, mrecv, {"slab": slab - mine + other})
+
+    for j in range(1, NEAR):
+        to_member(j).start()
+    send_tiles(0)
     tiles[0] = send[slab]
-    sums_in[0, 0:1] = sums_send[slab, 0:1]
+    sums_in[0] = sums_send[mine]
     total[...] = jnp.zeros_like(total)
     if len(waves) > 1:
         pl.semaphore_wait(ready.at[0], 2)
     for step in range(1, len(waves) - 1):
         announce(step)
+    if len(waves) > 1:
+        send_tiles(1)
     for halo in yhalos:
         halo.wait()
 
@@ -232,71 +242,83 @@
     sums = lax.fori_loop(1, cx - 1, plane, tuple(jnp.zeros((1, nz), F32) for c in range(3)))
     for step in range(1, len(waves) - 1):
         pl.semaphore_wait(ready.at[step], 2)
-    far_first(1, n_slab - 1, send_sums)
-    for wave in range(len(waves)):
-        send_tiles(wave)
+        send_tiles(step + 1)
     for halo in xhalos:
         halo.wait()
     field[:, 0] = jnp.where(slab > 0, field[:, 0], 0.0)
     field[:, cx + 1] = jnp.where(slab < n_slab - 1, field[:, cx + 1], 0.0)
     sums = lax.fori_loop(0, 2, lambda i, sums: plane(i * (cx - 1), sums), sums)
-    all_sums = remote(sums_send.at[1:n_slab, 0:1], sums_in.at[1:n_slab, 0:1], msend, mrecv, s_up)
+    width = sums_in.shape[2]
+    group = jnp.where(iota((nz, width), 0) // CB == iota((nz, width), 1) % levels, 1.0, 0.0)
+    stacked = jnp.concatenate(list(sums) + [jnp.zeros((5, nz), F32)], axis=0)
+    spread = jnp.dot(stacked, group, precision=HIGH, preferred_element_type=F32)
+    sublane, lane = iota((8, width), 0), iota((8, width), 1)
+    own_line = jnp.sum(jnp.where((lane // levels == sublane) & (sublane < 3), spread, 0.0), axis=0, keepdims=True)
+    all_sums = remote(sums_send.at[1:NEAR], sums_in.at[1:NEAR], msend, mrecv, s_up)
     all_sums.wait_recv()
-    line = jnp.sum(sums_in[:, 0, :], axis=0, keepdims=True)
-    width = sums_in.shape[2]
-    row, column = iota((8, width), 0), iota((8, width), 1)
-    tile_rows = jnp.where((column // levels == row) & (row < 3), line, 0.0)
-    place = jnp.where(iota((width, lanes), 0) % levels + pencil * levels == iota((width, lanes), 1), 1.0, 0.0)
-    group = jnp.where(iota((nz, lanes), 0) // CB + pencil * levels == iota((nz, lanes), 1), 1.0, 0.0)
-    stacked = jnp.concatenate(list(sums) + [jnp.zeros((5, nz), F32)], axis=0)
-    moment[...] = jnp.dot(
-        jnp.concatenate([stacked, tile_rows], axis=1), jnp.concatenate([group, place], axis=0),
-        precision=HIGH, preferred_element_type=F32,
-    )
-
-    far_first(1, n_pencil - 1, lambda i: remote(moment, inbox.at[i], asend, arecv, pencil_peer(i)).start())
-    inbox[0] = moment[...]
-    arrived = remote(inbox.at[1:n_pencil], inbox.at[1:n_pencil], asend, arecv, p_up)
+    message[...] = jnp.sum(sums_in[...], axis=0) + jnp.where(sublane == slab // NEAR, own_line, 0.0)
+    far_first(1, n_slab - 1, lambda i: remote(message, everywhere.at[slab], bsend, brecv, slab_peer(i)).start())
+    everywhere[slab] = message[...]
+    gathered = remote(everywhere.at[1:n_slab], everywhere.at[1:n_slab], bsend, brecv, s_up)
+
+    shape = (8, lanes)
+    rel_x = [((slab - iota(shape, 0) * NEAR - x) * cx).astype(F32) for x in range(NEAR)]
+    rel_y = ((iota(shape, 1) // levels - pencil) * cy).astype(F32)
+    target_level = iota(shape, 1) % levels
+
+    def rel_z(level):
+        return ((target_level - level) * CB).astype(F32)
+
+    def prepare(level, carry):
+        along_z = rel_z(level)
+        flat_sq = rel_y * rel_y + along_z * along_z + sigma * sigma
+        for x in range(NEAR):
+            inverse = lax.rsqrt(rel_x[x] * rel_x[x] + flat_sq)
+            kern[level * NEAR + x] = inverse * inverse * inverse
+        return carry
+
+    lax.fori_loop(0, levels, prepare, 0)
     groups = tiles.shape[0] * 4 * tiles.shape[2] // lhs.shape[1]
     early = max(1, len(waves) - 1)
     for wave in range(early):
         tiles_of(wave).wait_recv()
-    deposit(tiles, lhs, rhs, total, 0, groups // 4)
-    arrived.wait_recv()
-    slab_moment[...] = jnp.sum(inbox[...], axis=0)
-    far_first(1, n_slab - 1, lambda i: remote(slab_moment, everywhere.at[slab], bsend, brecv, slab_peer(i)).start())
-    everywhere[slab] = slab_moment[...]
-    gathered = remote(everywhere.at[1:n_slab], everywhere.at[1:n_slab], bsend, brecv, s_up)
-    deposit(tiles, lhs, rhs, total, groups // 4, groups // 2)
+    deposit(tiles, lhs, rhs, total, 0, groups // 2)
     for wave in range(early, len(waves)):
         tiles_of(wave).wait_recv()
-    deposit(tiles, lhs, rhs, total, groups // 2, groups)
+    cut = groups * BEFORE // 8
+    deposit(tiles, lhs, rhs, total, groups // 2, cut)
+
+    gathered.wait_recv()
+    moments = []
+    for x in range(NEAR):
+        rows = everywhere[x]
+        for z in range(1, n_slab // NEAR):
+            rows = rows + everywhere[z * NEAR + x]
+        moments.append(rows)
+    sums = [jnp.zeros(shape, F32) for c in range(3)]
+    for level in range(levels):
+        along_z = rel_z(level)
+        for x in range(NEAR):
+            m0, m1, m2 = (moments[x][:, c * levels + level : c * levels + level + 1] for c in range(3))
+            weight = kern[level * NEAR + x]
+            sums[0] += weight * (along_z * m1 - rel_y * m2)
+            sums[1] += weight * (rel_x[x] * m2 - along_z * m0)
+            sums[2] += weight * (rel_y * m0 - rel_x[x] * m1)
+    lines = [jnp.sum(part, axis=0, keepdims=True) for part in sums]
+    partial[...] = jnp.concatenate(lines + [jnp.zeros((5, lanes), F32)], axis=0)
+    far_first(1, n_pencil - 1, lambda i: remote(partial, inbox.at[i], asend, arecv, pencil_peer(i)).start())
+    inbox[0] = partial[...]
+    arrived = remote(inbox.at[1:n_pencil], inbox.at[1:n_pencil], asend, arecv, p_up)
+
+    deposit(tiles, lhs, rhs, total, cut, groups)
+    stores = [pltpu.make_async_copy(out.at[c], out_hbm.at[c], out_sem.at[c]) for c in range(3)]
     for c in range(3):
         out[c] += total[c * cx * cy : (c + 1) * cx * cy].reshape(cx, cy, nz)
-    stores = [pltpu.make_async_copy(out.at[c], out_hbm.at[c], out_sem.at[c]) for c in range(3)]
-    for store in stores:
-        store.start()
-    gathered.wait_recv()
-
-    shape = (n_slab, lanes)
-    rel_x = ((slab - iota(shape, 0)) * cx).astype(F32)
-    rel_y = ((pencil - iota(shape, 1) // levels) * cy).astype(F32)
-    level = iota(shape, 1) % levels
-    plane_sq = rel_x * rel_x + rel_y * rel_y + sigma * sigma
-    m0, m1, m2 = (everywhere[:, c, :] for c in range(3))
-    fixed = (-(rel_y * m2), rel_x * m2, rel_y * m0 - rel_x * m1)
-    far_sums = ([], [], [])
-    for target in range(levels):
-        rel_z = ((target - level) * CB).astype(F32)
-        inverse = lax.rsqrt(plane_sq + rel_z * rel_z)
-        weight = inverse * inverse * inverse
-        terms = (rel_z * m1 + fixed[0], fixed[1] - rel_z * m0, fixed[2])
-        for c in range(3):
-            far_sums[c].append(jnp.sum(weight * terms[c], axis=0, keepdims=True))
-    ones = jnp.ones((8, lanes), F32)
+        stores[c].start()
+    arrived.wait_recv()
+    result = pltpu.roll(jnp.sum(inbox[...], axis=0), lax.rem(lanes - pencil * levels, lanes), 1)
     for c in range(3):
-        rows = jnp.concatenate(far_sums[c], axis=0)
-        far[c, 0] = lax.dot_general(ones, rows, (((1,), (1,)), ((), ())), precision=HIGH, preferred_element_type=F32)[0:1]
+        far[c, 0] = result[c : c + 1, 0:levels]
     all_sums.wait_send()
     for wave in range(len(waves)):
         tiles_of(wave).wait_send()
@@ -306,15 +328,7 @@
         store.wait()
 
 
-def hand_out_kernel(field, far, field_out, far_out, sem):
-    copies = [pltpu.make_async_copy(field.at[c], field_out.at[c], sem.at[c]) for c in range(3)]
-    for copy in copies:
-        copy.start()
-    far_out[...] = far[...]
-    for copy in copies:
-        copy.wait()
-
-
+BEFORE = 5
 NEAR = 4
 GROUP = 4
 
@@ -329,7 +343,7 @@
     smem = pl.BlockSpec(memory_space=pltpu.SMEM)
     dma = pltpu.SemaphoreType.DMA
     outs = (jax.ShapeDtypeStruct(vorticity.shape, F32), jax.ShapeDtypeStruct((3, 1, 1, levels), F32))
-    field, far = pl.pallas_call(
+    return pl.pallas_call(
         functools.partial(step_kernel, n_slab, n_pencil, float(cx * n_slab // 4)),
         out_shape=outs,
         in_specs=[hbm, hbm, hbm, hbm, hbm, vmem, smem],
@@ -340,18 +354,19 @@
             pltpu.VMEM((n_tiles, tile_len), jnp.int32),
             pltpu.VMEM((n_slab, 8, tile_len), F32),
             pltpu.VMEM((n_slab, 8, tile_len), F32),
-            pltpu.VMEM((n_slab, 8, tile_len), F32),
-            pltpu.VMEM((n_slab, 8, tile_len), F32),
+            pltpu.VMEM((NEAR, 8, tile_len), F32),
+            pltpu.VMEM((NEAR, 8, tile_len), F32),
             pltpu.VMEM((2, FIELDS, cx, nz), F32),
             pltpu.VMEM((2, FIELDS, cx, nz), F32),
             pltpu.VMEM((3 * cx * cy, GROUP * 4 * tile_len), BF16),
             pltpu.VMEM((nz, GROUP * 4 * tile_len), BF16),
             pltpu.VMEM((3 * cx * cy, nz), F32),
             pltpu.VMEM((3, cx, cy, nz), F32),
+            pltpu.VMEM((8, tile_len), F32),
+            pltpu.VMEM((n_slab, 8, tile_len), F32),
+            pltpu.VMEM((levels * NEAR, 8, lanes), F32),
             pltpu.VMEM((8, lanes), F32),
             pltpu.VMEM((n_pencil, 8, lanes), F32),
-            pltpu.VMEM((8, lanes), F32),
-            pltpu.VMEM((n_slab, 8, lanes), F32),
             dma((5,)), dma((2,)), dma((2,)), dma((2,)), dma((2,)), dma((4,)), dma((4,)), dma, dma, dma, dma, dma, dma,
             pltpu.SemaphoreType.REGULAR((4,)), dma((3,)),
         ],
@@ -361,15 +376,6 @@
         vorticity, velocity, viscosity, jnp.transpose(tile_weights, (1, 0, 2)), tile_cells,
         tile_dest.reshape(1, -1), tile_count,
     )
-    return pl.pallas_call(
-        hand_out_kernel,
-        out_shape=outs,
-        in_specs=[hbm, vmem],
-        out_specs=(hbm, vmem),
-        scratch_shapes=[dma((3,))],
-        compiler_params=pltpu.CompilerParams(vmem_limit_bytes=VMEM_LIMIT),
-        name="hand_out",
-    )(field, far)
 
 
 def solution(mesh):

time: 60.5 us -> 37.5 us (0.62)
  Pallas kernels: 58.8 us -> 33.4 us
  local copies, waits for them, and re-layouts: 0 us -> 2.66 us
    pallas_call x1 -> x0, Pallas kernels: 26.2 us -> none  [per_device(): pl.pallas_call(hand_out_kernel, out_shape=outs, in_specs=[hbm, vmem], out...]
    unnamed x0 -> x4, local copies, waits for them, and re-layouts: none -> 2.66 us
    pallas_call x1, Pallas kernels: 32.6 us -> 33.4 us  [per_device(): pl.pallas_call(functools.partial(step_kernel, n_slab, n_pencil, float(cx...]
where the time goes in v4:
time: 37.5 us; the launch traced here: 37.3 us
  Pallas kernels  33.4 us (89%)
  local copies, waits for them, and re-layouts  2.66 us (7%)
  between operations  1.3 us (3%)
    pallas_call x1, Pallas kernels, per_device(): pl.pallas_call(functools.partial(step_kernel, n_slab, n_pencil, float(cx...  33.4 us
    unnamed x4, local copies, waits for them, and re-layouts  2.66 us

profile of v4, /device:TPU:1, one launch (start us, length us, event | category | flops | bytes accessed | tf_op | source)
XLA Modules:
  0.0 37.3 jit_solution(8116428465131897207)
XLA Ops:
  1.3 33.4 %step.1 = (f32[3,8,32,256]{3,2,1,0:T(8,128)}, f32[3,1,1,16]{3,2,1,0:T(1,128)}) custom-call(f32[3,8,32,256]{3,2,1,0:T(8,128)} %vort.1, f32[3,8,32,256]{3,2,1,0:T(8,128)} %velo.1, f32[8,32,256]{2,1,0:T(8,128)} %visc.1, f32[3,32,128]{2,1,0:T(8,128)} %bitcast.2, s32[32,128]{1,0:T(8,128)} %cells.1, s32[1,32]{1,0:T(1,128)} %bitcast.3, s32[1]{0:T(128)S(6)} %copy.11.count), custom_call_target="tpu_custom_call" | custom-call | tf_op jit(solution)/shard_map/step/pallas_call | solution.py:346
  34.7 0.0 copy-start
  34.7 2.1 %copy.12 = f32[3,8,32,256]{3,2,1,0:T(8,128)} copy(f32[3,8,32,256]{3,2,1,0:T(8,128)} %get-tuple-element.4) | data formatting | bytes 1572864
  36.8 0.0 copy-done
  36.8 0.6 %copy.13 = f32[3,1,1,16]{3,2,1,0:T(1,128)} copy(f32[3,1,1,16]{3,2,1,0:T(1,128)S(1)} %copy-done) | data formatting | bytes 384
Async XLA Ops:
  34.7 2.1 %copy-start = (f32[3,1,1,16]{3,2,1,0:T(1,128)S(1)}, f32[3,1,1,16]{3,2,1,0:T(1,128)}, u32[]{:S(2)}) copy-start(f32[3,1,1,16]{3,2,1,0:T(1,128)} %get-tuple-element.5) | copy-start | bytes 580

commit v5 on v4

--- a/solution.py
+++ b/solution.py
@@ -102,8 +102,8 @@
 def step_kernel(
     n_slab, n_pencil, sigma, vort, velo, visc, weights, cells, dest, count,
     out_hbm, far,
-    field, wtile, ctile, send, tiles, sums_send, sums_in, yface, yhalo, lhs, rhs, total, out, message, everywhere, kern,
-    partial, inbox, load_sem, xsend, xrecv, ysend, yrecv, tsend, trecv, msend, mrecv, asend, arecv, bsend, brecv, ready, out_sem,
+    field, wtile, ctile, send, tiles, sums_send, sums_in, yface, yhalo, lhs, rhs, total, out, message, everywhere, beside,
+    kern, partial, inbox, load_sem, xsend, xrecv, xsend2, xrecv2, ysend, yrecv, tsend, trecv, msend, mrecv, asend, arecv, bsend, brecv, ready, out_sem,
 ):
     slab, pencil = lax.axis_index("slab"), lax.axis_index("pencil")
     cx, cy, nz = out.shape[1], out.shape[2], out.shape[3]
@@ -150,10 +150,16 @@
         remote(yface.at[0], yhalo.at[1], ysend.at[0], yrecv.at[1], p_down),
         remote(yface.at[1], yhalo.at[0], ysend.at[1], yrecv.at[0], p_up),
     ]
-    xhalos = [
-        remote(field.at[:, 1], field.at[:, cx + 1], xsend.at[0], xrecv.at[1], s_down),
-        remote(field.at[:, cx], field.at[:, 0], xsend.at[1], xrecv.at[0], s_up),
-    ]
+    low, high = slice(0, cy // 2), slice(cy // 2, cy)
+
+    def face_halos(to_lower, to_upper, send_sem, recv_sem):
+        return [
+            remote(field.at[:, 1, to_lower], field.at[:, cx + 1, to_lower], send_sem.at[0], recv_sem.at[1], s_down),
+            remote(field.at[:, cx, to_upper], field.at[:, 0, to_upper], send_sem.at[1], recv_sem.at[0], s_up),
+        ]
+
+    xhalos = face_halos(high, low, xsend, xrecv)
+    xhalos2 = face_halos(low, high, xsend2, xrecv2)
     for halo in yhalos + xhalos:
         halo.start()
 
@@ -194,6 +200,7 @@
     tiles[0] = send[slab]
     sums_in[0] = sums_send[mine]
     total[...] = jnp.zeros_like(total)
+    beside[...] = jnp.zeros_like(beside)
     if len(waves) > 1:
         pl.semaphore_wait(ready.at[0], 2)
     for step in range(1, len(waves) - 1):
@@ -207,7 +214,7 @@
     first_row, last_row = row == 0, row == cy - 1
     has_before, has_after = pencil > 0, pencil < n_pencil - 1
 
-    def plane(x, sums):
+    def plane(x, sums, is_first=False, is_last=False):
         def ahead_y(c):
             edge = jnp.where(has_after, yhalo[1, c, pl.ds(x, 1), :], 0.0)
             return jnp.where(last_row, edge, pltpu.roll(field[c, x + 1], cy - 1, 0))
@@ -217,7 +224,10 @@
             return jnp.where(first_row, edge, pltpu.roll(field[c, x + 1], 1, 0))
 
         neighbours = [
-            (lambda c: field[c, x + 2], lambda c: field[c, x]),
+            (
+                (lambda c: 0.0) if is_last else (lambda c: field[c, x + 2]),
+                (lambda c: 0.0) if is_first else (lambda c: field[c, x]),
+            ),
             (ahead_y, behind_y),
             (lambda c: pltpu.roll(field[c, x + 1], nz - 1, 1), lambda c: pltpu.roll(field[c, x + 1], 1, 1)),
         ]
@@ -230,8 +240,10 @@
             face_behind = 0.5 * (own_visc + backward(6))
             for c in range(3):
                 change[c] += factor * (forward(3 + c) - backward(3 + c))
-                change[c] += face_ahead * (forward(c) - own[c])
-                change[c] += face_behind * (backward(c) - own[c])
+                if d > 0 or not is_last:
+                    change[c] += face_ahead * (forward(c) - own[c])
+                if d > 0 or not is_first:
+                    change[c] += face_behind * (backward(c) - own[c])
         result = []
         for c in range(3):
             value = own[c] + time_step * change[c]
@@ -239,27 +251,63 @@
             result.append(sums[c] + jnp.sum(value, axis=0, keepdims=True))
         return tuple(result)
 
+    def face(inner, outer, exists, sign, rows):
+        here = [field[c, inner, rows] for c in range(FIELDS)]
+        there = [jnp.where(exists, field[c, outer, rows], 0.0) for c in range(FIELDS)]
+        middle = 0.5 * (here[6] + there[6])
+        for_here, for_there = [], []
+        for c in range(3):
+            flow = middle * (there[c] - here[c])
+            for_here.append(time_step * (sign * (0.5 * here[0]) * there[3 + c] + flow))
+            for_there.append(jnp.where(exists, time_step * (-sign * (0.5 * there[0]) * here[3 + c] - flow), 0.0))
+        return for_here, for_there
+
+    def rim(inner, exists, rows):
+        viscous = 0.5 * time_step * field[6, inner, rows]
+        return [jnp.where(exists, 0.0, -viscous * field[c, inner, rows]) for c in range(3)]
+
+    def over_rows(values):
+        return [jnp.sum(value, axis=0, keepdims=True) for value in values]
+
     sums = lax.fori_loop(1, cx - 1, plane, tuple(jnp.zeros((1, nz), F32) for c in range(3)))
+    sums = plane(0, sums, is_first=True)
+    sums = plane(cx - 1, sums, is_last=True)
+    has_lower, has_upper = slab > 0, slab < n_slab - 1
+    rims = [over_rows(rim(1, has_lower, high)), over_rows(rim(cx, has_upper, low))]
+    sums = [sums[c] + rims[0][c] + rims[1][c] for c in range(3)]
     for step in range(1, len(waves) - 1):
         pl.semaphore_wait(ready.at[step], 2)
         send_tiles(step + 1)
     for halo in xhalos:
         halo.wait()
-    field[:, 0] = jnp.where(slab > 0, field[:, 0], 0.0)
-    field[:, cx + 1] = jnp.where(slab < n_slab - 1, field[:, cx + 1], 0.0)
-    sums = lax.fori_loop(0, 2, lambda i, sums: plane(i * (cx - 1), sums), sums)
+    lower_own, lower_other = map(over_rows, face(1, 0, has_lower, -1.0, low))
+    upper_own, upper_other = map(over_rows, face(cx, cx + 1, has_upper, 1.0, high))
+    sums = [sums[c] + lower_own[c] + upper_own[c] for c in range(3)]
     width = sums_in.shape[2]
     group = jnp.where(iota((nz, width), 0) // CB == iota((nz, width), 1) % levels, 1.0, 0.0)
-    stacked = jnp.concatenate(list(sums) + [jnp.zeros((5, nz), F32)], axis=0)
+    stacked = jnp.concatenate(sums + upper_other + lower_other + [jnp.zeros((7, nz), F32)], axis=0)
     spread = jnp.dot(stacked, group, precision=HIGH, preferred_element_type=F32)
-    sublane, lane = iota((8, width), 0), iota((8, width), 1)
-    own_line = jnp.sum(jnp.where((lane // levels == sublane) & (sublane < 3), spread, 0.0), axis=0, keepdims=True)
+    sublane, lane = iota((16, width), 0), iota((16, width), 1)
+    part, third = lane // levels % 4, lane // (width // 2)
+
+    def line(mask):
+        return jnp.sum(jnp.where(mask, spread, 0.0), axis=0, keepdims=True)
+
+    own_line = line((third == 0) & (part < 3) & (sublane == part))
+    beside_line = line((part < 3) & (sublane == 3 + 3 * third + part))
     all_sums = remote(sums_send.at[1:NEAR], sums_in.at[1:NEAR], msend, mrecv, s_up)
     all_sums.wait_recv()
-    message[...] = jnp.sum(sums_in[...], axis=0) + jnp.where(sublane == slab // NEAR, own_line, 0.0)
-    far_first(1, n_slab - 1, lambda i: remote(message, everywhere.at[slab], bsend, brecv, slab_peer(i)).start())
-    everywhere[slab] = message[...]
-    gathered = remote(everywhere.at[1:n_slab], everywhere.at[1:n_slab], bsend, brecv, s_up)
+    rows = jnp.sum(sums_in[...], axis=0) + jnp.where(iota((8, width), 0) == slab // NEAR, own_line, 0.0)
+    message[0:4] = rows[0:4] + pltpu.roll(rows, width // 2, 1)[4:8]
+    message[4:5] = beside_line
+    far_first(
+        1, n_slab - 1,
+        lambda i: remote(message.at[0:5], everywhere.at[slab, 0:5], bsend, brecv, slab_peer(i)).start(),
+    )
+    for halo in xhalos2:
+        halo.start()
+    everywhere[slab, 0:5] = message[0:5]
+    gathered = remote(everywhere.at[1:n_slab, 0:5], everywhere.at[1:n_slab, 0:5], bsend, brecv, s_up)
 
     shape = (8, lanes)
     rel_x = [((slab - iota(shape, 0) * NEAR - x) * cx).astype(F32) for x in range(NEAR)]
@@ -289,12 +337,16 @@
     deposit(tiles, lhs, rhs, total, groups // 2, cut)
 
     gathered.wait_recv()
+    beside[8 : 8 + n_slab, :] = everywhere[:, 4, :]
     moments = []
     for x in range(NEAR):
-        rows = everywhere[x]
+        rows = everywhere[x, 0:4]
         for z in range(1, n_slab // NEAR):
-            rows = rows + everywhere[z * NEAR + x]
-        moments.append(rows)
+            rows = rows + everywhere[z * NEAR + x, 0:4]
+        rows = jnp.concatenate([rows, pltpu.roll(rows, width // 2, 1)], axis=0)
+        from_lower = beside[pl.ds(7 + x, 8, stride=NEAR), :]
+        from_upper = beside[pl.ds(9 + x, 8, stride=NEAR), :]
+        moments.append(rows + from_lower + pltpu.roll(from_upper, width // 2, 1))
     sums = [jnp.zeros(shape, F32) for c in range(3)]
     for level in range(levels):
         along_z = rel_z(level)
@@ -311,6 +363,13 @@
     arrived = remote(inbox.at[1:n_pencil], inbox.at[1:n_pencil], asend, arecv, p_up)
 
     deposit(tiles, lhs, rhs, total, cut, groups)
+    for halo in xhalos2:
+        halo.wait()
+    everything = slice(0, cy)
+    for x, inner, outer, exists, sign in ((0, 1, 0, has_lower, -1.0), (cx - 1, cx, cx + 1, has_upper, 1.0)):
+        terms, _ = face(inner, outer, exists, sign, everything)
+        for c in range(3):
+            out[c, x] += terms[c]
     stores = [pltpu.make_async_copy(out.at[c], out_hbm.at[c], out_sem.at[c]) for c in range(3)]
     for c in range(3):
         out[c] += total[c * cx * cy : (c + 1) * cx * cy].reshape(cx, cy, nz)
@@ -364,10 +423,11 @@
             pltpu.VMEM((3, cx, cy, nz), F32),
             pltpu.VMEM((8, tile_len), F32),
             pltpu.VMEM((n_slab, 8, tile_len), F32),
+            pltpu.VMEM((8 * NEAR + 16, tile_len), F32),
             pltpu.VMEM((levels * NEAR, 8, lanes), F32),
             pltpu.VMEM((8, lanes), F32),
             pltpu.VMEM((n_pencil, 8, lanes), F32),
-            dma((5,)), dma((2,)), dma((2,)), dma((2,)), dma((2,)), dma((4,)), dma((4,)), dma, dma, dma, dma, dma, dma,
+            dma((5,)), dma((2,)), dma((2,)), dma((2,)), dma((2,)), dma((2,)), dma((2,)), dma((4,)), dma((4,)), dma, dma, dma, dma, dma, dma,
             pltpu.SemaphoreType.REGULAR((4,)), dma((3,)),
         ],
         compiler_params=pltpu.CompilerParams(collective_id=0, has_side_effects=True, vmem_limit_bytes=VMEM_LIMIT),

time: 37.5 us -> 32.5 us (0.87)
  Pallas kernels: 33.4 us -> 28.4 us
    pallas_call x1, Pallas kernels: 33.4 us -> 28.4 us  [per_device(): pl.pallas_call(functools.partial(step_kernel, n_slab, n_pencil, float(cx...]
where the time goes in v5:
time: 32.5 us; the launch traced here: 32.3 us
  Pallas kernels  28.4 us (87%)
  local copies, waits for them, and re-layouts  2.66 us (8%)
  between operations  1.3 us (4%)
    pallas_call x1, Pallas kernels, per_device(): pl.pallas_call(functools.partial(step_kernel, n_slab, n_pencil, float(cx...  28.4 us
    unnamed x4, local copies, waits for them, and re-layouts  2.66 us

profile of v5, /device:TPU:1, one launch (start us, length us, event | category | flops | bytes accessed | tf_op | source)
XLA Modules:
  0.0 32.3 jit_solution(2268551023779310573)
XLA Ops:
  1.3 28.4 %step.1 = (f32[3,8,32,256]{3,2,1,0:T(8,128)}, f32[3,1,1,16]{3,2,1,0:T(1,128)}) custom-call(f32[3,8,32,256]{3,2,1,0:T(8,128)} %vort.1, f32[3,8,32,256]{3,2,1,0:T(8,128)} %velo.1, f32[8,32,256]{2,1,0:T(8,128)} %visc.1, f32[3,32,128]{2,1,0:T(8,128)} %bitcast.2, s32[32,128]{1,0:T(8,128)} %cells.1, s32[1,32]{1,0:T(1,128)} %bitcast.3, s32[1]{0:T(128)S(6)} %copy.11.count), custom_call_target="tpu_custom_call" | custom-call | tf_op jit(solution)/shard_map/step/pallas_call | solution.py:405
  29.7 0.0 copy-start
  29.7 2.1 %copy.12 = f32[3,8,32,256]{3,2,1,0:T(8,128)} copy(f32[3,8,32,256]{3,2,1,0:T(8,128)} %get-tuple-element.4) | data formatting | bytes 1572864
  31.8 0.0 copy-done
  31.8 0.6 %copy.13 = f32[3,1,1,16]{3,2,1,0:T(1,128)} copy(f32[3,1,1,16]{3,2,1,0:T(1,128)S(1)} %copy-done) | data formatting | bytes 384
Async XLA Ops:
  29.7 2.1 %copy-start = (f32[3,1,1,16]{3,2,1,0:T(1,128)S(1)}, f32[3,1,1,16]{3,2,1,0:T(1,128)}, u32[]{:S(2)}) copy-start(f32[3,1,1,16]{3,2,1,0:T(1,128)} %get-tuple-element.5) | copy-start | bytes 580

commit v6 on v5

--- a/solution.py
+++ b/solution.py
@@ -109,7 +109,7 @@
     cx, cy, nz = out.shape[1], out.shape[2], out.shape[3]
     lanes = partial.shape[1]
     levels = nz // CB
-    waves = [min(2 * NEAR, n_slab - 1)]
+    waves = [min(2 * GREET, n_slab - 1)]
     while waves[-1] < n_slab - 1:
         waves.append(min(2 * waves[-1], n_slab - 1))
 
@@ -201,12 +201,10 @@
     sums_in[0] = sums_send[mine]
     total[...] = jnp.zeros_like(total)
     beside[...] = jnp.zeros_like(beside)
-    if len(waves) > 1:
-        pl.semaphore_wait(ready.at[0], 2)
     for step in range(1, len(waves) - 1):
+        pl.semaphore_wait(ready.at[step - 1], 2)
         announce(step)
-    if len(waves) > 1:
-        send_tiles(1)
+        send_tiles(step)
     for halo in yhalos:
         halo.wait()
 
@@ -269,15 +267,16 @@
     def over_rows(values):
         return [jnp.sum(value, axis=0, keepdims=True) for value in values]
 
-    sums = lax.fori_loop(1, cx - 1, plane, tuple(jnp.zeros((1, nz), F32) for c in range(3)))
+    sums = lax.fori_loop(1, SPLIT, plane, tuple(jnp.zeros((1, nz), F32) for c in range(3)))
+    if len(waves) > 1:
+        pl.semaphore_wait(ready.at[len(waves) - 2], 2)
+        send_tiles(len(waves) - 1)
+    sums = lax.fori_loop(SPLIT, cx - 1, plane, sums)
     sums = plane(0, sums, is_first=True)
     sums = plane(cx - 1, sums, is_last=True)
     has_lower, has_upper = slab > 0, slab < n_slab - 1
     rims = [over_rows(rim(1, has_lower, high)), over_rows(rim(cx, has_upper, low))]
     sums = [sums[c] + rims[0][c] + rims[1][c] for c in range(3)]
-    for step in range(1, len(waves) - 1):
-        pl.semaphore_wait(ready.at[step], 2)
-        send_tiles(step + 1)
     for halo in xhalos:
         halo.wait()
     lower_own, lower_other = map(over_rows, face(1, 0, has_lower, -1.0, low))
@@ -357,10 +356,10 @@
             sums[1] += weight * (rel_x[x] * m2 - along_z * m0)
             sums[2] += weight * (rel_y * m0 - rel_x[x] * m1)
     lines = [jnp.sum(part, axis=0, keepdims=True) for part in sums]
-    partial[...] = jnp.concatenate(lines + [jnp.zeros((5, lanes), F32)], axis=0)
-    far_first(1, n_pencil - 1, lambda i: remote(partial, inbox.at[i], asend, arecv, pencil_peer(i)).start())
-    inbox[0] = partial[...]
-    arrived = remote(inbox.at[1:n_pencil], inbox.at[1:n_pencil], asend, arecv, p_up)
+    partial[0:4] = jnp.concatenate(lines + [jnp.zeros((1, lanes), F32)], axis=0)
+    far_first(1, n_pencil - 1, lambda i: remote(partial.at[0:4], inbox.at[i, 0:4], asend, arecv, pencil_peer(i)).start())
+    inbox[0, 0:4] = partial[0:4]
+    arrived = remote(inbox.at[1:n_pencil, 0:4], inbox.at[1:n_pencil, 0:4], asend, arecv, p_up)
 
     deposit(tiles, lhs, rhs, total, cut, groups)
     for halo in xhalos2:
@@ -375,7 +374,7 @@
         out[c] += total[c * cx * cy : (c + 1) * cx * cy].reshape(cx, cy, nz)
         stores[c].start()
     arrived.wait_recv()
-    result = pltpu.roll(jnp.sum(inbox[...], axis=0), lax.rem(lanes - pencil * levels, lanes), 1)
+    result = pltpu.roll(jnp.sum(inbox[:, 0:4, :], axis=0), lax.rem(lanes - pencil * levels, lanes), 1)
     for c in range(3):
         far[c, 0] = result[c : c + 1, 0:levels]
     all_sums.wait_send()
@@ -389,6 +388,8 @@
 
 BEFORE = 5
 NEAR = 4
+GREET = 4
+SPLIT = 4
 GROUP = 4
 
 

time: 32.5 us -> 32.4 us (level)
  no operation moved by 1% of the time
where the time goes in v6:
time: 32.4 us; the launch traced here: 32.2 us
  Pallas kernels  28.3 us (87%)
  local copies, waits for them, and re-layouts  2.66 us (8%)
  between operations  1.3 us (4%)
    pallas_call x1, Pallas kernels, per_device(): pl.pallas_call(functools.partial(step_kernel, n_slab, n_pencil, float(cx...  28.3 us
    unnamed x4, local copies, waits for them, and re-layouts  2.66 us

profile of v6, /device:TPU:1, one launch (start us, length us, event | category | flops | bytes accessed | tf_op | source)
XLA Modules:
  0.0 32.2 jit_solution(6615946437791479837)
XLA Ops:
  1.3 28.3 %step.1 = (f32[3,8,32,256]{3,2,1,0:T(8,128)}, f32[3,1,1,16]{3,2,1,0:T(1,128)}) custom-call(f32[3,8,32,256]{3,2,1,0:T(8,128)} %vort.1, f32[3,8,32,256]{3,2,1,0:T(8,128)} %velo.1, f32[8,32,256]{2,1,0:T(8,128)} %visc.1, f32[3,32,128]{2,1,0:T(8,128)} %bitcast.2, s32[32,128]{1,0:T(8,128)} %cells.1, s32[1,32]{1,0:T(1,128)} %bitcast.3, s32[1]{0:T(128)S(6)} %copy.11.count), custom_call_target="tpu_custom_call" | custom-call | tf_op jit(solution)/shard_map/step/pallas_call | solution.py:406
  29.5 0.0 copy-start
  29.5 2.1 %copy.12 = f32[3,8,32,256]{3,2,1,0:T(8,128)} copy(f32[3,8,32,256]{3,2,1,0:T(8,128)} %get-tuple-element.4) | data formatting | bytes 1572864
  31.6 0.0 copy-done
  31.6 0.6 %copy.13 = f32[3,1,1,16]{3,2,1,0:T(1,128)} copy(f32[3,1,1,16]{3,2,1,0:T(1,128)S(1)} %copy-done) | data formatting | bytes 384
Async XLA Ops:
  29.5 2.1 %copy-start = (f32[3,1,1,16]{3,2,1,0:T(1,128)S(1)}, f32[3,1,1,16]{3,2,1,0:T(1,128)}, u32[]{:S(2)}) copy-start(f32[3,1,1,16]{3,2,1,0:T(1,128)} %get-tuple-element.5) | copy-start | bytes 580

commit v7 on v6

--- a/solution.py
+++ b/solution.py
@@ -37,6 +37,25 @@
     return pltpu.make_async_remote_copy(
         src_ref=src, dst_ref=dst, send_sem=send_sem, recv_sem=recv_sem, device_id=device, device_id_type=MESH
     )
+
+
+def pieces(values):
+    first = values.astype(BF16)
+    rest = values - first.astype(F32)
+    second = rest.astype(BF16)
+    return [first, second, (rest - second.astype(F32)).astype(BF16)]
+
+
+def pick_dot(ones, values):
+    width = values.shape[1]
+    wide = jnp.dot(ones.astype(BF16), jnp.concatenate(pieces(values), axis=1), preferred_element_type=F32)
+    return wide[:, 0:width] + wide[:, width : 2 * width] + wide[:, 2 * width :]
+
+
+def dot_pick(values, ones):
+    rows = values.shape[0]
+    tall = jnp.dot(jnp.concatenate(pieces(values), axis=0), ones.astype(BF16), preferred_element_type=F32)
+    return tall[0:rows] + tall[rows : 2 * rows] + tall[2 * rows :]
 
 
 def pack_tiles(weights, cells, dest, live, send, sums, nz):
@@ -51,7 +70,7 @@
         pick = jnp.where(before == j, match, 0.0)
         for c in range(4):
             rows = weights[c] if c < 3 else (cells[...] + 1).astype(F32)
-            send[:, 4 * j + c, :] = jnp.dot(pick, rows, precision=HIGH, preferred_element_type=F32)
+            send[:, 4 * j + c, :] = pick_dot(pick, rows)
     levels = nz // CB
     level = (cells[...] & (nz - 1)) // CB
     lane = iota((tiles, lanes), 1)
@@ -64,7 +83,7 @@
     row = iota((NEAR * 8, tiles), 0)
     member = jnp.where(row % 8 < n_slab // NEAR, row % 8 * NEAR + row // 8, -1)
     match = jnp.where((dest[...] == member) & (iota((NEAR * 8, tiles), 1) < live), 1.0, 0.0)
-    added = jnp.dot(match, by_level, precision=HIGH, preferred_element_type=F32)
+    added = pick_dot(match, by_level)
     sums[...] = added.reshape(NEAR, 8, lanes)
 
 
@@ -285,7 +304,7 @@
     width = sums_in.shape[2]
     group = jnp.where(iota((nz, width), 0) // CB == iota((nz, width), 1) % levels, 1.0, 0.0)
     stacked = jnp.concatenate(sums + upper_other + lower_other + [jnp.zeros((7, nz), F32)], axis=0)
-    spread = jnp.dot(stacked, group, precision=HIGH, preferred_element_type=F32)
+    spread = dot_pick(stacked, group)
     sublane, lane = iota((16, width), 0), iota((16, width), 1)
     part, third = lane // levels % 4, lane // (width // 2)
 

time: 32.4 us -> 32.3 us (level)
  no operation moved by 1% of the time
where the time goes in v7:
time: 32.3 us; the launch traced here: 32.2 us
  Pallas kernels  28.2 us (87%)
  local copies, waits for them, and re-layouts  2.66 us (8%)
  between operations  1.3 us (4%)
    pallas_call x1, Pallas kernels, per_device(): pl.pallas_call(functools.partial(step_kernel, n_slab, n_pencil, float(cx...  28.2 us
    unnamed x4, local copies, waits for them, and re-layouts  2.66 us

profile of v7, /device:TPU:1, one launch (start us, length us, event | category | flops | bytes accessed | tf_op | source)
XLA Modules:
  0.0 32.2 jit_solution(12293885503591106273)
XLA Ops:
  1.3 28.2 %step.1 = (f32[3,8,32,256]{3,2,1,0:T(8,128)}, f32[3,1,1,16]{3,2,1,0:T(1,128)}) custom-call(f32[3,8,32,256]{3,2,1,0:T(8,128)} %vort.1, f32[3,8,32,256]{3,2,1,0:T(8,128)} %velo.1, f32[8,32,256]{2,1,0:T(8,128)} %visc.1, f32[3,32,128]{2,1,0:T(8,128)} %bitcast.2, s32[32,128]{1,0:T(8,128)} %cells.1, s32[1,32]{1,0:T(1,128)} %bitcast.3, s32[1]{0:T(128)S(6)} %copy.11.count), custom_call_target="tpu_custom_call" | custom-call | tf_op jit(solution)/shard_map/step/pallas_call | solution.py:425
  29.5 0.0 copy-start
  29.5 2.1 %copy.12 = f32[3,8,32,256]{3,2,1,0:T(8,128)} copy(f32[3,8,32,256]{3,2,1,0:T(8,128)} %get-tuple-element.4) | data formatting | bytes 1572864
  31.6 0.0 copy-done
  31.6 0.6 %copy.13 = f32[3,1,1,16]{3,2,1,0:T(1,128)} copy(f32[3,1,1,16]{3,2,1,0:T(1,128)S(1)} %copy-done) | data formatting | bytes 384
Async XLA Ops:
  29.5 2.1 %copy-start = (f32[3,1,1,16]{3,2,1,0:T(1,128)S(1)}, f32[3,1,1,16]{3,2,1,0:T(1,128)}, u32[]{:S(2)}) copy-start(f32[3,1,1,16]{3,2,1,0:T(1,128)} %get-tuple-element.5) | copy-start | bytes 580

commit v8 on v7

--- a/solution.py
+++ b/solution.py
@@ -147,15 +147,15 @@
         pltpu.make_async_copy(weights, wtile, load_sem.at[3]),
         pltpu.make_async_copy(cells, ctile, load_sem.at[4]),
     ]
+    barrier = pltpu.get_barrier_semaphore()
+
+    def greet(where):
+        pl.semaphore_signal(barrier, inc=1, device_id=where, device_id_type=MESH)
+
+    far_first(1, waves[0], lambda i: greet(slab_peer(i)))
+    far_first(1, n_pencil - 1, lambda i: greet(pencil_peer(i)))
     for load in loads + tile_loads:
         load.start()
-    barrier = pltpu.get_barrier_semaphore()
-
-    def greet(where):
-        pl.semaphore_signal(barrier, inc=1, device_id=where, device_id_type=MESH)
-
-    far_first(1, waves[0], lambda i: greet(slab_peer(i)))
-    far_first(1, n_pencil - 1, lambda i: greet(pencil_peer(i)))
     for load in loads:
         load.wait()
     for c in range(FIELDS):

time: 32.3 us -> 32.3 us (level)
  no operation moved by 1% of the time
where the time goes in v8:
time: 32.3 us; the launch traced here: 32.2 us
  Pallas kernels  28.2 us (87%)
  local copies, waits for them, and re-layouts  2.66 us (8%)
  between operations  1.3 us (4%)
    pallas_call x1, Pallas kernels, per_device(): pl.pallas_call(functools.partial(step_kernel, n_slab, n_pencil, float(cx...  28.2 us
    unnamed x4, local copies, waits for them, and re-layouts  2.66 us

profile of v8, /device:TPU:1, one launch (start us, length us, event | category | flops | bytes accessed | tf_op | source)
XLA Modules:
  0.0 32.2 jit_solution(16782930630937097546)
XLA Ops:
  1.3 28.2 %step.1 = (f32[3,8,32,256]{3,2,1,0:T(8,128)}, f32[3,1,1,16]{3,2,1,0:T(1,128)}) custom-call(f32[3,8,32,256]{3,2,1,0:T(8,128)} %vort.1, f32[3,8,32,256]{3,2,1,0:T(8,128)} %velo.1, f32[8,32,256]{2,1,0:T(8,128)} %visc.1, f32[3,32,128]{2,1,0:T(8,128)} %bitcast.2, s32[32,128]{1,0:T(8,128)} %cells.1, s32[1,32]{1,0:T(1,128)} %bitcast.3, s32[1]{0:T(128)S(6)} %copy.11.count), custom_call_target="tpu_custom_call" | custom-call | tf_op jit(solution)/shard_map/step/pallas_call | solution.py:425
  29.5 0.0 copy-start
  29.5 2.1 %copy.12 = f32[3,8,32,256]{3,2,1,0:T(8,128)} copy(f32[3,8,32,256]{3,2,1,0:T(8,128)} %get-tuple-element.4) | data formatting | bytes 1572864
  31.6 0.0 copy-done
  31.6 0.6 %copy.13 = f32[3,1,1,16]{3,2,1,0:T(1,128)} copy(f32[3,1,1,16]{3,2,1,0:T(1,128)S(1)} %copy-done) | data formatting | bytes 384
Async XLA Ops:
  29.5 2.1 %copy-start = (f32[3,1,1,16]{3,2,1,0:T(1,128)S(1)}, f32[3,1,1,16]{3,2,1,0:T(1,128)}, u32[]{:S(2)}) copy-start(f32[3,1,1,16]{3,2,1,0:T(1,128)} %get-tuple-element.5) | copy-start | bytes 580
